TPU v7x, 128 devices: a whole 4x4x4 slice. The times are simulated.
128 devices in a mesh: wide: 64 (over z, y, x_hi, core), narrow: 2 (over x_lo).
Axes of the slice: x: 4 (x_hi: 2, x_lo: 2; x = x_hi * 2 + x_lo), y: 4, z: 4, core: 2. Of those that a mesh axis runs over, the one named last changes fastest.
Arguments:
- layer_in: bfloat16 [8192, 1536], P('wide'), may hold values from -16 to 16
- lengths: int32 [4], replicated, may hold values from 1 to 8127, as said below
- norm_attn: float32 [1536], replicated, may hold values from 0.1 to 1.9
- w_qkv: bfloat16 [1536, 2048], P(None, 'narrow'), may hold values from -0.15625 to 0.15625
- qkv_bias: float32 [2, 1024], P('narrow'), may hold values from -3 to 3
- w_out: bfloat16 [1536, 1536], P('narrow'), may hold values from -4 to 4
- norm_mlp: float32 [1536], replicated, may hold values from 0.1 to 1.9
- w_gate: bfloat16 [1536, 8960], P(None, 'narrow'), may hold values from -0.15625 to 0.15625
- w_up: bfloat16 [1536, 8960], P(None, 'narrow'), may hold values from -0.15625 to 0.15625
- w_down: bfloat16 [8960, 1536], P('narrow'), may hold values from -0.0625 to 0.0625
- out_grad: bfloat16 [8192, 1536], P('wide'), may hold values from -16 to 16
Outputs:
- layer_out: bfloat16 [8192, 1536], P('wide')
- in_grad: bfloat16 [8192, 1536], P('wide')
- grad_norm_attn: float32 [1536], P('wide')
- grad_qkv: float32 [1536, 2048], P('wide', 'narrow')
- grad_bias: float32 [2, 7, 128], P('narrow', None, 'wide')
- grad_value_bias: float32 [2, 128], P('narrow', 'wide')
- grad_out: float32 [1536, 1536], P('narrow', 'wide')
- grad_norm_mlp: float32 [1536], P('wide')
- grad_gate: float32 [1536, 8960], P('wide', 'narrow')
- grad_up: float32 [1536, 8960], P('wide', 'narrow')
- grad_down: float32 [8960, 1536], P('narrow', 'wide')
Inputs may be any that keep to these rules, and one draw needn't show every extreme that they name: 4 sequences packed one after another; their lengths sum to 8192; one of them, which one is drawn, reaches from the first token shard of wide to the last.
All inputs are finite; a program needn't handle non-finite values.
Results may differ from a plain program's by a relative error of at most 0.022.
Values may be sent and summed in bfloat16 or wider, within the bound.
A program may use at most 384 MiB of HBM per device.

v0:
```python
import math

import jax
import jax.numpy as jnp
from jax import lax
from jax.sharding import Mesh
from jax.sharding import PartitionSpec as P

HD = 128
QH = 12
KVH = 2
WIDE = ("wide_0", "wide_1", "wide_2", "wide_3")


rms_eps = 1e-06
rope_base = 10000.0
big_negative = -1e30
highest = lax.Precision.HIGHEST


def copy_for_each(array, axis):
    peers = lax.axis_size(axis)
    return lax.all_to_all(
        jnp.broadcast_to(array[None], (peers, *array.shape)), axis, 0, 0, tiled=True
    )


def in_order(parts, dim):
    parts = jnp.moveaxis(parts, 0, dim)
    shape = parts.shape
    return parts.reshape(*shape[:dim], shape[dim] * shape[dim + 1], *shape[dim + 2 :])


def gathered_by_axis(array, axes, dim):
    far, near = axes
    parts = copy_for_each(copy_for_each(array, far), near)
    return in_order(parts.swapaxes(0, 1).reshape(-1, *array.shape), dim)


def sent_together(arrays, axis, dim, along):
    ends, at = ([], 0)
    for a in arrays[:-1]:
        at += a.shape[along]
        ends.append(at)
    both = jnp.concatenate(arrays, axis=along)
    return tuple(jnp.split(gathered_by_axis(both, axis, dim), ends, axis=along))


def over_copies(array, axis):
    return copy_for_each(array, axis).astype(jnp.float32).sum(axis=0)


def split_up(array, dim, peers):
    shape = array.shape
    parts = array.reshape(*shape[:dim], peers, shape[dim] // peers, *shape[dim + 1 :])
    return jnp.moveaxis(parts, dim, 0)


def summed_on_arrival(array, axis, dim):
    parts = split_up(array, dim, lax.axis_size(axis))
    arrived = lax.all_to_all(parts, axis, split_axis=0, concat_axis=0, tiled=True)
    return arrived.sum(axis=0)


def sum_by_axis(array, axes, dim):
    far, near = axes
    own = summed_on_arrival(split_up(array, dim, lax.axis_size(far)), near, dim + 1)
    return jnp.sum(lax.all_to_all(own, far, 0, 0, tiled=True), axis=0)


def side_by_side(arrays, axis, dim, along):
    both = jnp.concatenate(arrays, axis=along)
    out, at, finished = (sum_by_axis(both, axis, dim), 0, [])
    for a in arrays:
        finished.append(lax.slice_in_dim(out, at, at + a.shape[along], axis=along))
        at += a.shape[along]
    return tuple(finished)


def dot_first(left, right):
    return lax.dot_general(
        left, right, (((0,), (0,)), ((), ())), preferred_element_type=jnp.float32
    )


def dot_last(left, right):
    return lax.dot_general(
        left, right, (((1,), (1,)), ((), ())), preferred_element_type=jnp.float32
    )


def row_starts(lengths, token_ids):
    ends = jnp.cumsum(lengths)
    before = ends[None, :] <= token_ids[:, None]
    return jnp.sum(jnp.where(before, lengths[None, :], 0), axis=1)


def rope_tables(positions, head_size):
    half_size = head_size // 2
    freqs = rope_base ** (-2.0 * jnp.arange(half_size, dtype=jnp.float32) / head_size)
    angles = positions.astype(jnp.float32)[:, None] * freqs[None, :]
    return (jnp.cos(angles), jnp.sin(angles))


def rotate(values, cosine, sine):
    half_size = values.shape[-1] // 2
    first_half = values[..., :half_size]
    second_half = values[..., half_size:]
    cos_heads = cosine[:, None, :]
    sin_heads = sine[:, None, :]
    return jnp.concatenate(
        [
            first_half * cos_heads - second_half * sin_heads,
            second_half * cos_heads + first_half * sin_heads,
        ],
        axis=-1,
    )


def unrotate(grads, cosine, sine):
    half_size = grads.shape[-1] // 2
    first_half = grads[..., :half_size]
    second_half = grads[..., half_size:]
    cos_heads = cosine[:, None, :]
    sin_heads = sine[:, None, :]
    return jnp.concatenate(
        [
            first_half * cos_heads + second_half * sin_heads,
            second_half * cos_heads - first_half * sin_heads,
        ],
        axis=-1,
    )


def normalize(values):
    inverse = lax.rsqrt(jnp.mean(values * values, axis=-1) + rms_eps)
    return (values * inverse[:, None], inverse)


def norm_back(grad_normed, normed, inverse):
    inner = jnp.mean(grad_normed * normed, axis=-1, keepdims=True)
    return inverse[:, None] * (grad_normed - normed * inner)


def shards(
    layer_in, lengths, norm_attn, w_qkv, qkv_bias, w_out, norm_mlp, w_gate, w_up, w_down, out_grad
):
    tok_rows = layer_in.shape[0]
    group_heads = QH // KVH
    query_width = group_heads * HD
    query_count = tok_rows * group_heads
    first_tok = lax.axis_index(WIDE) * tok_rows
    own_ids = first_tok + jnp.arange(tok_rows, dtype=jnp.int32)
    seq_starts = row_starts(lengths, own_ids)
    cosine, sine = rope_tables(own_ids - seq_starts, HD)
    scale = HD ** (-0.5)
    input_f32 = layer_in.astype(jnp.float32)
    normed_attn, inverse_attn = normalize(input_f32)
    act_attn = (normed_attn * norm_attn).astype(jnp.bfloat16)
    projected = jnp.dot(act_attn, w_qkv, preferred_element_type=jnp.float32) + qkv_bias[0]
    queries = rotate(projected[:, :query_width].reshape(tok_rows, group_heads, HD), cosine, sine)
    queries = queries.astype(jnp.bfloat16).reshape(query_count, HD)
    key_own = rotate(
        projected[:, query_width : query_width + HD].reshape(tok_rows, 1, HD), cosine, sine
    )
    key_own = key_own.astype(jnp.bfloat16).reshape(tok_rows, HD)
    value_own = projected[:, query_width + HD :].astype(jnp.bfloat16)
    key_all, value_all = sent_together(
        (key_own, value_own), (("wide_0", "wide_1", "wide_2"), "wide_3"), 0, 1
    )
    key_total = key_all.shape[0]
    block_size = math.gcd(512, key_total)
    query_ids = jnp.repeat(own_ids, group_heads, total_repeat_length=query_count)
    query_starts = jnp.repeat(seq_starts, group_heads, total_repeat_length=query_count)
    first_block = seq_starts[0] // block_size
    end_block = (first_tok + tok_rows - 1) // block_size + 1

    def block_scores(block_index):
        key_block = lax.dynamic_slice_in_dim(key_all, block_index * block_size, block_size, 0)
        value_block = lax.dynamic_slice_in_dim(value_all, block_index * block_size, block_size, 0)
        scores = dot_last(queries, key_block) * scale
        key_ids = block_index * block_size + jnp.arange(block_size, dtype=jnp.int32)
        allowed = (key_ids[None, :] <= query_ids[:, None]) & (
            key_ids[None, :] >= query_starts[:, None]
        )
        return (scores, allowed, key_block, value_block)

    def stats_step(block_index, carried):
        running_max, running_sum = carried
        scores, allowed, unused_key, unused_value = block_scores(block_index)
        new_max = jnp.maximum(
            running_max, jnp.max(jnp.where(allowed, scores, big_negative), axis=1)
        )
        weights = jnp.where(allowed, jnp.exp(scores - new_max[:, None]), 0.0)
        return (new_max, running_sum * jnp.exp(running_max - new_max) + jnp.sum(weights, axis=1))

    start_stats = (
        jnp.full((query_count,), big_negative, jnp.float32),
        jnp.zeros((query_count,), jnp.float32),
    )
    final_max, final_sum = lax.fori_loop(first_block, end_block, stats_step, start_stats)
    log_total = final_max + jnp.log(final_sum)

    def block_probs(block_index):
        scores, allowed, key_block, value_block = block_scores(block_index)
        return (
            jnp.where(allowed, jnp.exp(scores - log_total[:, None]), 0.0),
            key_block,
            value_block,
        )

    def value_step(block_index, accums):
        rounded_acc, exact_acc = accums
        probs, unused_key, value_block = block_probs(block_index)
        rounded_acc = rounded_acc + jnp.dot(
            probs.astype(jnp.bfloat16), value_block, preferred_element_type=jnp.float32
        )
        exact_acc = exact_acc + jnp.dot(probs, value_block.astype(jnp.float32), precision=highest)
        return (rounded_acc, exact_acc)

    zero_rows = jnp.zeros((query_count, HD), jnp.float32)
    attn_rows, exact_rows = lax.fori_loop(
        first_block, end_block, value_step, (zero_rows, zero_rows)
    )
    attn_low = attn_rows.astype(jnp.bfloat16).reshape(tok_rows, query_width)
    attn_out = over_copies(
        jnp.dot(attn_low, w_out, preferred_element_type=jnp.float32).astype(jnp.bfloat16), "narrow"
    ).astype(jnp.float32)
    resid = input_f32 + attn_out
    normed_mlp, inverse_mlp = normalize(resid)
    act_mlp = (normed_mlp * norm_mlp).astype(jnp.bfloat16)
    gate_proj = jnp.dot(act_mlp, w_gate, preferred_element_type=jnp.float32)
    up_proj = jnp.dot(act_mlp, w_up, preferred_element_type=jnp.float32)
    sigmoid_gate = jax.nn.sigmoid(gate_proj)
    silu_gate = gate_proj * sigmoid_gate
    hidden = (silu_gate * up_proj).astype(jnp.bfloat16)
    mlp_out = over_copies(
        jnp.dot(hidden, w_down, preferred_element_type=jnp.float32).astype(jnp.bfloat16), "narrow"
    ).astype(jnp.float32)
    layer_out = (resid + mlp_out).astype(jnp.bfloat16)
    grad_down = dot_first(hidden, out_grad)
    grad_hidden = dot_last(out_grad, w_down)
    grad_gate_pre = (
        grad_hidden * up_proj * (sigmoid_gate * (1.0 + gate_proj * (1.0 - sigmoid_gate)))
    ).astype(jnp.bfloat16)
    grad_up_pre = (grad_hidden * silu_gate).astype(jnp.bfloat16)
    grad_gate = dot_first(act_mlp, grad_gate_pre)
    grad_up = dot_first(act_mlp, grad_up_pre)
    grad_act_mlp = over_copies(
        (dot_last(grad_gate_pre, w_gate) + dot_last(grad_up_pre, w_up)).astype(jnp.bfloat16),
        "narrow",
    ).astype(jnp.float32)
    grad_norm_mlp = jnp.sum(grad_act_mlp * normed_mlp, axis=0)
    grad_resid = out_grad.astype(jnp.float32) + norm_back(
        grad_act_mlp * norm_mlp, normed_mlp, inverse_mlp
    )
    grad_branch = grad_resid.astype(jnp.bfloat16)
    grad_wout = dot_first(attn_low, grad_branch)
    grad_attn = dot_last(grad_branch, w_out).astype(jnp.bfloat16).reshape(query_count, HD)
    balance = jnp.sum(grad_attn.astype(jnp.float32) * exact_rows, axis=1)

    def grad_terms(block_index):
        probs, key_block, value_block = block_probs(block_index)
        dprobs = dot_last(grad_attn, value_block)
        grad_scores = (probs * (dprobs - balance[:, None]) * scale).astype(jnp.bfloat16)
        return (probs, grad_scores, key_block)

    zero_queries = jnp.zeros((query_count, HD), jnp.float32)

    def back_step(block_index, carried):
        grad_q, grad_k, grad_v = carried
        probs, grad_scores, key_block = grad_terms(block_index)
        grad_q = grad_q + jnp.dot(grad_scores, key_block, preferred_element_type=jnp.float32)
        offset = block_index * block_size
        old_k = lax.dynamic_slice_in_dim(grad_k, offset, block_size, 0)
        old_v = lax.dynamic_slice_in_dim(grad_v, offset, block_size, 0)
        grad_k = lax.dynamic_update_slice_in_dim(
            grad_k, old_k + dot_first(grad_scores, queries), offset, 0
        )
        grad_v = lax.dynamic_update_slice_in_dim(
            grad_v, old_v + dot_first(probs.astype(jnp.bfloat16), grad_attn), offset, 0
        )
        return (grad_q, grad_k, grad_v)

    zero_keys = jnp.zeros((key_total, HD), jnp.float32)
    grad_q, grad_k_all, grad_v_all = lax.fori_loop(
        first_block, end_block, back_step, (zero_queries, zero_keys, zero_keys)
    )
    grad_key, grad_value = side_by_side(
        (grad_k_all, grad_v_all), (("wide_0", "wide_1", "wide_2"), "wide_3"), 0, 1
    )
    grad_query_pre = unrotate(grad_q.reshape(tok_rows, group_heads, HD), cosine, sine).reshape(
        tok_rows, query_width
    )
    grad_key_pre = unrotate(grad_key.reshape(tok_rows, 1, HD), cosine, sine).reshape(tok_rows, HD)
    grad_projected = jnp.concatenate([grad_query_pre, grad_key_pre, grad_value], axis=1).astype(
        jnp.bfloat16
    )
    bias_grid = jnp.sum(grad_projected.astype(jnp.float32), axis=0).reshape(1, group_heads + 2, HD)
    bias_front = bias_grid[:, : group_heads + 1]
    bias_value = bias_grid[:, group_heads + 1]
    grad_wqkv = dot_first(act_attn, grad_projected)
    grad_act_attn = over_copies(
        dot_last(grad_projected, w_qkv).astype(jnp.bfloat16), "narrow"
    ).astype(jnp.float32)
    grad_norm_attn = jnp.sum(grad_act_attn * normed_attn, axis=0)
    in_grad = (grad_resid + norm_back(grad_act_attn * norm_attn, normed_attn, inverse_attn)).astype(
        jnp.bfloat16
    )
    (
        sum_qkv,
        sum_out,
        sum_front,
        sum_value,
        sum_norm_attn,
        sum_gate,
        sum_up,
        sum_down,
        sum_norm_mlp,
    ) = (
        lax.psum_scatter(grad_wqkv, WIDE, scatter_dimension=0, tiled=True),
        lax.psum_scatter(grad_wout, WIDE, scatter_dimension=1, tiled=True),
        lax.psum_scatter(bias_front, WIDE, scatter_dimension=2, tiled=True),
        lax.psum_scatter(bias_value, WIDE, scatter_dimension=1, tiled=True),
        lax.psum_scatter(grad_norm_attn, WIDE, scatter_dimension=0, tiled=True),
        lax.psum_scatter(grad_gate, WIDE, scatter_dimension=0, tiled=True),
        lax.psum_scatter(grad_up, WIDE, scatter_dimension=0, tiled=True),
        lax.psum_scatter(grad_down, WIDE, scatter_dimension=1, tiled=True),
        lax.psum_scatter(grad_norm_mlp, WIDE, scatter_dimension=0, tiled=True),
    )
    return (
        layer_out,
        in_grad,
        sum_norm_attn,
        sum_qkv,
        sum_front,
        sum_value,
        sum_out,
        sum_norm_mlp,
        sum_gate,
        sum_up,
        sum_down,
    )


def solution(mesh):
    torus = Mesh(
        mesh.devices.reshape(4, 4, 2, 2, mesh.shape["narrow"]),
        ("wide_0", "wide_1", "wide_2", "wide_3", "narrow"),
    )
    in_specs = (
        P(WIDE, None),
        P(),
        P(),
        P(None, "narrow"),
        P("narrow", None),
        P("narrow", None),
        P(),
        P(None, "narrow"),
        P(None, "narrow"),
        P("narrow", None),
        P(WIDE, None),
    )
    out_specs = (
        P(WIDE, None),
        P(WIDE, None),
        P(WIDE),
        P(WIDE, "narrow"),
        P("narrow", None, WIDE),
        P("narrow", WIDE),
        P("narrow", WIDE),
        P(WIDE),
        P(WIDE, "narrow"),
        P(WIDE, "narrow"),
        P("narrow", WIDE),
    )
    return jax.shard_map(
        shards, mesh=torus, in_specs=in_specs, out_specs=out_specs, check_vma=False
    )
```

profile of v0, /device:TPU:1, one launch (start us, length us, event | category | flops | bytes accessed | tf_op | source)
XLA Modules:
  0.0 1457.5 jit_solution(15520432550203024914)
XLA Ops:
  14.1 11.6 all-to-all-start
  25.9 4.8 gather_fusion.1
  43.1 12.0 all-to-all-done
  57.2 8.9 all_to_all.40
  72.2 6.1 while.41
  84.5 13.5 all_to_all.42
  99.4 8.9 fusion.65
  111.8 12.2 multiply_convert_fusion
  123.9 9.8 fusion.66
  133.8 9.4 fusion.24
  148.6 8.0 convolution_convert_fusion.1
  168.1 5.2 all-to-all-done.3
  187.6 8.4 while.42
  201.0 14.5 all_to_all.41
  215.5 6.5 reduce_sum.152
  222.0 252.8 %all-to-all-start.6 = ((f32[32,128,256]{2,1,0:T(8,128)}), f32[32,128,256]{2,1,0:T(8,128)}, u32[]{:S(2)}, u32[]{:S(2)}) async-start(f32[32,128,256]{2,1,0:T(8,128)} %reduce_sum.152), calls=%async_computation.6 | async-start | bytes 8388608 | tf_op jit(solution)/shard_map/all_to_all | solution.py:68
  482.2 49.5 %all-to-all-done.6 = f32[32,128,256]{2,1,0:T(8,128)} async-done(((f32[32,128,256]{2,1,0:T(8,128)}), f32[32,128,256]{2,1,0:T(8,128)}, u32[]{:S(2)}, u32[]{:S(2)}) %all-to-all-start.6) | async-done | bytes 4194336 | tf_op jit(solution)/shard_map/all_to_all | solution.py:68
  546.4 14.5 fusion.68
  561.0 14.8 %fusion.67 = f32[1536,4480]{1,0:T(8,128)} fusion(bf16[128,1536]{1,0:T(8,128)(2,1)} %copy-done.9, bf16[128,4480]{1,0:T(8,128)(2,1)} %copy-done.20), kind=kOutput, calls=%fused_computation.139 | convolution fusion | flops 1761607680 | bytes 29065216 | tf_op jit(solution)/shard_map/dot_general | solution.py:81
  576.2 14.8 %fusion.69 = f32[4480,1536]{0,1:T(8,128)} fusion(bf16[128,4480]{1,0:T(8,128)(2,1)} %get-tuple-element.327, bf16[128,1536]{1,0:T(8,128)(2,1)} %param.33), kind=kOutput, calls=%fused_computation.141 | convolution fusion | flops 1761607680 | bytes 29065216 | tf_op jit(solution)/shard_map/dot_general | solution.py:81
  611.9 325.4 %all-reduce.7 = (f32[1536]{0:T(1024)}, f32[1,7,128]{1,0,2:T(1,128)}, f32[1,128]{1,0:T(1,128)}, f32[1536]{0:T(1024)}) all-reduce(f32[1536]{0:T(1024)} %get-tuple-element.253, f32[1,7,128]{1,0,2:T(1,128)} %copy.59, ...), channel_id=2, replica_groups=mesh['wide_0'=4,'wide_1'=4,'wide_2'=2,'wide_3'=2,'narrow'=2] {'wide_0','..., use_global_device_ids=true, to_apply=%region_22.24.clone | all-reduce | flops 4096 | bytes 32768
  945.4 8.2 reduce-scatter.19.cloned.1.call-done
  953.6 248.7 %reduce-scatter.17.cloned.1.call-done = f32[24,4480]{1,0:T(8,128)} async-done(((f32[1536,4480]{1,0:T(8,128)}), f32[24,4480]{1,0:T(8,128)}) %reduce-scatter.17.cloned.1.call-update) | async-done | bytes 430096
  1202.3 248.4 %reduce-scatter.21.cloned.1.call-done = f32[4480,24]{0,1:T(8,128)} async-done(((f32[4480,1536]{0,1:T(8,128)}), f32[4480,24]{0,1:T(8,128)}) %reduce-scatter.21.cloned.1.call-update) | async-done | bytes 430096
  (203 shorter events, 140.8 us)
Async XLA Ops:
  14.1 11.8 copy-start.35
  14.1 41.0 %all-to-all-start = ((bf16[32,128,256]{2,1,0:T(8,128)(2,1)}), bf16[32,128,256]{2,1,0:T(8,128)(2,1)}, u32[]{:S(2)}, u32[]{:S(2)}) async-start(bf16[32,128,256]{2,1,0:T(8,128)(2,1)} %broadcast_in_dim.52), calls=%async_computation | async-start | bytes 4194304 | tf_op jit(solution)/shard_map/all_to_all | solution.py:23
  82.0 26.3 %slice-start = ((s8[13762560]{0:T(1024)(128)(4,1)}), s8[4194304]{0:T(1024)(128)(4,1)S(1)}, s32[]{:S(2)}) async-start(s8[13762560]{0:T(1024)(128)(4,1)} %bitcast.117), calls=%async_computation.18 | async-start | bytes 8388608
  84.4 13.7 copy-start.7
  98.1 10.2 slice-start.1
  99.4 8.9 copy-start.9
  99.4 8.9 slice-start.2
  123.9 9.9 copy-start.20
  123.9 9.9 copy-start.21
  144.1 14.2 all-to-all-start.4
  160.2 13.1 all-to-all-start.3
  164.5 780.9 %reduce-scatter.15.cloned.1.call-start = ((), (), s32[]{:S(2)}) async-start(), calls=%async_computation.14 | async-start | bytes 4792320 | tf_op jit(solution)/shard_map/reduce_scatter | solution.py:322
  222.0 253.1 %copy-start.3 = (f32[768,128]{1,0:T(8,128)S(1)}, f32[768,128]{1,0:T(8,128)}, u32[]{:S(2)}) copy-start(f32[768,128]{1,0:T(8,128)} %get-tuple-element.204) | copy-start | bytes 1179652
  222.0 309.8 %all-to-all-start.6 = ((f32[32,128,256]{2,1,0:T(8,128)}), f32[32,128,256]{2,1,0:T(8,128)}, u32[]{:S(2)}, u32[]{:S(2)}) async-start(f32[32,128,256]{2,1,0:T(8,128)} %reduce_sum.152), calls=%async_computation.6 | async-start | bytes 8388608 | tf_op jit(solution)/shard_map/all_to_all | solution.py:68
  474.8 470.6 %reduce-scatter.13.cloned.1.call-start = ((), (), s32[]{:S(2)}) async-start(), calls=%async_computation.13 | async-start | bytes 6389760 | tf_op jit(solution)/shard_map/reduce_scatter | solution.py:321
  482.2 56.4 %copy-start.33 = (f32[64]{0:T(128)S(1)}, f32[64]{0:T(128)}, u32[]{:S(2)}) copy-start(f32[64]{0:T(128)} %copy-done.32) | copy-start | bytes 772
  482.2 59.5 %copy-start.8 = (bf16[128,1536]{1,0:T(8,128)(2,1)S(1)}, bf16[128,1536]{1,0:T(8,128)(2,1)}, u32[]{:S(2)}) copy-start(bf16[128,1536]{1,0:T(8,128)(2,1)} %param.23) | copy-start | bytes 1179652
  482.2 59.5 %copy-start.25 = (f32[1536]{0:T(1024)S(1)}, f32[1536]{0:T(1024)}, u32[]{:S(2)}) copy-start(f32[1536]{0:T(1024)} %param.25) | copy-start | bytes 18436
  482.2 59.5 %copy-start.31 = (f32[128]{0:T(128)S(1)}, f32[128]{0:T(128)}, u32[]{:S(2)}) copy-start(f32[128]{0:T(128)} %copy-done.30) | copy-start | bytes 1540
  546.4 407.2 %reduce-scatter.19.cloned.1.call-start = ((), (), s32[]{:S(2)}) async-start(), calls=%async_computation.16 | async-start | bytes 27955200
  561.0 641.3 %reduce-scatter.17.cloned.1.call-start = ((), (), s32[]{:S(2)}) async-start(), calls=%async_computation.15 | async-start | bytes 27955200
  575.9 874.8 %reduce-scatter.21.cloned.1.call-start = ((), (), s32[]{:S(2)}) async-start(), calls=%async_computation.17 | async-start | bytes 27955200
  594.1 17.8 %copy-start.29 = (f32[1536]{0:T(1024)S(1)}, f32[1536]{0:T(1024)}, u32[]{:S(2)}) copy-start(f32[1536]{0:T(1024)} %get-tuple-element.251) | copy-start | bytes 18436
  594.1 14.1 all-to-all-start.7
  (28 other events, 66.0 us)
Sparse Core Ops, SparseCore 0:
  181.3 270.2 reduce-scatter.14
  546.5 157.4 reduce-scatter.12
  710.8 242.7 reduce-scatter.18
  960.3 242.0 reduce-scatter.16
  1209.0 241.7 reduce-scatter.20
where the time goes:
time: 1470 us; the launch traced here: 1460 us
  waiting for transfers between devices  576 us (39%)
  blocking collectives  362 us (25%)
  starting transfers between devices  278 us (19%)
  matrix products  126 us (9%)
  local copies, waits for them, and re-layouts  57.6 us (4%)
  other arithmetic  40.9 us (3%)
  between operations  16.1 us (1%)
    unnamed x8, waiting for transfers between devices  505 us
    unnamed x1, blocking collectives  325 us
    all_to_all x1, starting transfers between devices, sum_by_axis(): return jnp.sum(lax.all_to_all(own, far, 0, 0, tiled=True), axis=0)  253 us
    dot_general x7, matrix products, dot_first(): lax.dot_general(left, right, (((0,), (0,)), ((), ())), preferred_element_...  56 us
    all_to_all x1, waiting for transfers between devices, sum_by_axis(): return jnp.sum(lax.all_to_all(own, far, 0, 0, tiled=True), axis=0)  49.5 us
    dot_general x9, matrix products, dot_last(): lax.dot_general(left, right, (((1,), (1,)), ((), ())), preferred_element_...  40.2 us
  transfers between devices with their start and end apart: 10, of which 8 were waited for; matrix products, arithmetic and copies ran while one was open for 10% of the time, Pallas kernels for 0%

commit v1 on v0

v1 whole, which is shorter than its diff:
```python
import functools
import math

import jax
import jax.numpy as jnp
from jax import lax
from jax.experimental import pallas as pl
from jax.experimental.pallas import tpu as pltpu
from jax.sharding import Mesh
from jax.sharding import PartitionSpec as P

HD = 128
QH = 12
KVH = 2
HEADS = QH // KVH
D = 1536
FF = 8960
TOK = 128
TOKENS = 8192
NQ = HEADS * TOK
GROUP = 8
UNITS = FF // 2 // GROUP
OUT_COLS = HEADS * HD // GROUP

AXES = ("z", "y", "xh", "c", "n")
SIZE = {"z": 4, "y": 4, "xh": 2, "c": 2, "n": 2}
WIDE = ("z", "y", "xh", "c")
MESH = pl.DeviceIdType.MESH

rms_eps = 1e-06
rope_base = 10000.0
big_negative = -1e30
SCALE = HD ** (-0.5)
SCALE_LOG2 = SCALE * math.log2(math.e)
KEY_BLOCK = 512
BLOCK_SHARDS = KEY_BLOCK // TOK
Q_CHUNK = 256

bf16 = jnp.bfloat16
f32 = jnp.float32
VMEM = pl.BlockSpec(memory_space=pltpu.VMEM)
SMEM = pl.BlockSpec(memory_space=pltpu.SMEM)
ANY = pl.BlockSpec(memory_space=pl.ANY)


def nn(a, b):
    return lax.dot_general(a, b, (((1,), (0,)), ((), ())), preferred_element_type=f32)


def nt(a, b):
    return lax.dot_general(a, b, (((1,), (1,)), ((), ())), preferred_element_type=f32)


def tn(a, b):
    return lax.dot_general(a, b, (((0,), (0,)), ((), ())), preferred_element_type=f32)


def here():
    return {a: lax.axis_index(a) for a in AXES}


def step(me, axis, by):
    return lax.rem(me[axis] + by, SIZE[axis])


def at(me, **moved):
    return tuple(step(me, a, moved[a]) if a in moved else me[a] for a in AXES)


def greet(peers):
    barrier = pltpu.get_barrier_semaphore()
    for p in peers:
        pl.semaphore_signal(barrier, inc=1, device_id=p, device_id_type=MESH)
    pl.semaphore_wait(barrier, len(peers))


class Copies:
    def __init__(self, send_sems, recv_sems):
        self.send_sems, self.recv_sems, self.used, self.started = send_sems, recv_sems, 0, []

    def make(self, src, dst, target):
        k = self.used
        self.used += 1
        return pltpu.make_async_remote_copy(
            src_ref=src,
            dst_ref=dst,
            send_sem=self.send_sems.at[k],
            recv_sem=self.recv_sems.at[k],
            device_id=target,
            device_id_type=MESH,
        )

    def send(self, src, dst, target):
        copy = self.make(src, dst, target)
        copy.start()
        self.started.append(copy)
        return copy

    def finish(self):
        for copy in self.started:
            copy.wait_send()


def sems(count):
    return [pltpu.SemaphoreType.DMA((count,)), pltpu.SemaphoreType.DMA((count,))]


def params(ident, mib=60):
    return pltpu.CompilerParams(
        collective_id=ident, has_side_effects=True, vmem_limit_bytes=mib * 2**20
    )


def kv_gather_kernel(x, o, send_sems, recv_sems):
    me = here()
    z, y, xh, c = me["z"], me["y"], me["xh"], me["c"]
    partner, across = at(me, c=1), at(me, xh=1)
    ys = {d: at(me, y=d) for d in (1, 2, 3)}
    zs = {d: at(me, z=d) for d in (1, 2, 3)}
    o[z, y, xh, c] = x[...]
    greet([partner, across, *ys.values(), *zs.values()])
    copies = Copies(send_sems, recv_sems)
    mine = o.at[z, y, xh, c]
    first = copies.send(mine, mine, across)
    to_core = [copies.send(mine, mine, partner)]
    first.wait_recv()
    theirs = o.at[z, y, 1 - xh, c]
    to_core.append(copies.send(theirs, theirs, partner))
    half = TOK // 2
    low, high = pl.ds(0, half), pl.ds(half, half)

    def slot(zi, yi, rows):
        return o.at[zi, yi, :, c, rows]

    first_low, first_high = {}, {}
    for d in (1, 3, 2):
        first_low[d] = copies.send(slot(z, y, low), slot(z, y, low), ys[d])
        first_high[d] = copies.send(slot(z, y, high), slot(z, y, high), zs[d])
    second_low, second_high = {}, {}
    for e in (0, 1, 3, 2):
        yi, zi = lax.rem(y + (4 - e), 4), lax.rem(z + (4 - e), 4)
        if e:
            first_low[e].wait_recv()
            to_core.append(copies.send(slot(z, yi, low), slot(z, yi, low), partner))
            first_high[e].wait_recv()
            to_core.append(copies.send(slot(zi, y, high), slot(zi, y, high), partner))
        for d in (1, 3, 2):
            second_low[e, d] = copies.send(slot(z, yi, low), slot(z, yi, low), zs[d])
            second_high[e, d] = copies.send(slot(zi, y, high), slot(zi, y, high), ys[d])
    for e in (0, 1, 3, 2):
        for d in (1, 3, 2):
            yi, zi = lax.rem(y + (4 - e), 4), lax.rem(z + (4 - e), 4)
            yd, zd = lax.rem(y + (4 - d), 4), lax.rem(z + (4 - d), 4)
            second_low[e, d].wait_recv()
            to_core.append(copies.send(slot(zd, yi, low), slot(zd, yi, low), partner))
            second_high[e, d].wait_recv()
            to_core.append(copies.send(slot(zi, yd, high), slot(zi, yd, high), partner))
    for copy in to_core:
        copy.wait_recv()
    copies.finish()


def kv_gather(kv):
    return pl.pallas_call(
        kv_gather_kernel,
        out_shape=jax.ShapeDtypeStruct((4, 4, 2, 2, TOK, 2 * HD), bf16),
        in_specs=[VMEM],
        out_specs=VMEM,
        scratch_shapes=sems(80),
        compiler_params=params(1),
    )(kv)


def kv_reduce_kernel(p, o, cb, s, r1a, r1b, ta, tb, r2a, r2b, u, r3, send_sems, recv_sems):
    me = here()
    z, y, xh, c = me["z"], me["y"], me["xh"], me["c"]
    partner, across = at(me, c=1), at(me, xh=1)
    ys = {d: at(me, y=d) for d in (1, 2, 3)}
    zs = {d: at(me, z=d) for d in (1, 2, 3)}
    greet([partner, across, *ys.values(), *zs.values()])
    copies = Copies(send_sems, recv_sems)
    half = TOK // 2
    low, high = pl.ds(0, half), pl.ds(half, half)
    cores = [
        copies.send(p.at[:, :, :, 1 - c, rows], cb.at[:, :, :, rows], partner)
        for rows in (low, high)
    ]
    first_a, first_b = {}, {}
    cores[0].wait_recv()
    for zi in range(4):
        s[zi, :, :, low] = (p[zi, :, :, c, low].astype(f32) + cb[zi, :, :, low].astype(f32)).astype(bf16)
    for d in (1, 3, 2):
        first_a[d] = copies.send(s.at[step(me, "z", d), :, :, low], r1a.at[d - 1], zs[d])
    cores[1].wait_recv()
    for zi in range(4):
        s[zi, :, :, high] = (p[zi, :, :, c, high].astype(f32) + cb[zi, :, :, high].astype(f32)).astype(bf16)
    for d in (1, 3, 2):
        first_b[d] = copies.send(s.at[:, step(me, "y", d), :, high], r1b.at[d - 1], ys[d])
    for d in (1, 3, 2):
        first_a[d].wait_recv()
    ta[...] = (s[z, :, :, low].astype(f32) + r1a[0].astype(f32) + r1a[1].astype(f32) + r1a[2].astype(f32)).astype(bf16)
    second_a, second_b = {}, {}
    for d in (1, 3, 2):
        second_a[d] = copies.send(ta.at[step(me, "y", d)], r2a.at[d - 1], ys[d])
    for d in (1, 3, 2):
        first_b[d].wait_recv()
    tb[...] = (s[:, y, :, high].astype(f32) + r1b[0].astype(f32) + r1b[1].astype(f32) + r1b[2].astype(f32)).astype(bf16)
    for d in (1, 3, 2):
        second_b[d] = copies.send(tb.at[step(me, "z", d)], r2b.at[d - 1], zs[d])
    for d in (1, 3, 2):
        second_a[d].wait_recv()
        second_b[d].wait_recv()
    ua = ta[y].astype(f32) + r2a[0].astype(f32) + r2a[1].astype(f32) + r2a[2].astype(f32)
    ub = tb[z].astype(f32) + r2b[0].astype(f32) + r2b[1].astype(f32) + r2b[2].astype(f32)
    u[:, low] = ua.astype(bf16)
    u[:, high] = ub.astype(bf16)
    last = copies.send(u.at[1 - xh], r3, across)
    last.wait_recv()
    o[...] = u[xh].astype(f32) + r3[...].astype(f32)
    copies.finish()


def kv_reduce(terms):
    half = TOK // 2
    wide = 2 * HD
    return pl.pallas_call(
        kv_reduce_kernel,
        out_shape=jax.ShapeDtypeStruct((TOK, wide), f32),
        in_specs=[VMEM],
        out_specs=VMEM,
        scratch_shapes=[
            pltpu.VMEM((4, 4, 2, TOK, wide), bf16),
            pltpu.VMEM((4, 4, 2, TOK, wide), bf16),
            pltpu.VMEM((3, 4, 2, half, wide), bf16),
            pltpu.VMEM((3, 4, 2, half, wide), bf16),
            pltpu.VMEM((4, 2, half, wide), bf16),
            pltpu.VMEM((4, 2, half, wide), bf16),
            pltpu.VMEM((3, 2, half, wide), bf16),
            pltpu.VMEM((3, 2, half, wide), bf16),
            pltpu.VMEM((2, TOK, wide), bf16),
            pltpu.VMEM((TOK, wide), bf16),
            *sems(16),
        ],
        compiler_params=params(2),
    )(terms)


def group_gather_kernel(count, *refs):
    xs, os, (send_sems, recv_sems, local_sems) = refs[:count], refs[count : 2 * count], refs[2 * count :]
    me = here()
    y, c = me["y"], me["c"]
    partner = at(me, c=1)
    ys = {d: at(me, y=d) for d in (1, 2, 3)}
    greet([partner, *ys.values()])
    copies = Copies(send_sems, recv_sems)
    arrive, to_core, local = {}, [], []
    for i, (x, o) in enumerate(zip(xs, os)):
        for d in (1, 3, 2):
            arrive[i, d] = copies.send(x, o.at[y, c], ys[d])
        to_core.append(copies.send(x, o.at[y, c], partner))
        local.append(pltpu.make_async_copy(x, o.at[y, c], local_sems.at[i]))
        local[-1].start()
    for i, o in enumerate(os):
        for d in (1, 3, 2):
            arrive[i, d].wait_recv()
            got = o.at[lax.rem(y + (4 - d), 4), c]
            to_core.append(copies.send(got, got, partner))
    for copy in to_core:
        copy.wait_recv()
    for copy in local:
        copy.wait()
    copies.finish()


def group_gather(ident, arrays):
    count = len(arrays)
    return pl.pallas_call(
        functools.partial(group_gather_kernel, count),
        out_shape=[jax.ShapeDtypeStruct((4, 2, *a.shape), a.dtype) for a in arrays],
        in_specs=[ANY] * count,
        out_specs=[ANY] * count,
        scratch_shapes=[*sems(7 * count), pltpu.SemaphoreType.DMA((count,))],
        compiler_params=params(ident),
    )(*arrays)


def group_swap_kernel(count, *refs):
    xs, os, (send_sems, recv_sems, local_sems) = refs[:count], refs[count : 2 * count], refs[2 * count :]
    me = here()
    y, c = me["y"], me["c"]
    moves = [(d, e) for d in (1, 3, 2, 0) for e in (0, 1) if d or e]
    greet([at(me, y=d, c=e) for d, e in moves])
    copies = Copies(send_sems, recv_sems)
    local = []
    for i, (x, o) in enumerate(zip(xs, os)):
        for d, e in moves:
            copies.send(x.at[step(me, "y", d), step(me, "c", e)], o.at[y, c], at(me, y=d, c=e))
        local.append(pltpu.make_async_copy(x.at[y, c], o.at[y, c], local_sems.at[i]))
        local[-1].start()
    for copy in local:
        copy.wait()
    for copy in copies.started:
        copy.wait_recv()
    copies.finish()


def group_swap(ident, arrays):
    count = len(arrays)
    return pl.pallas_call(
        functools.partial(group_swap_kernel, count),
        out_shape=[jax.ShapeDtypeStruct(a.shape, a.dtype) for a in arrays],
        in_specs=[ANY] * count,
        out_specs=[ANY] * count,
        scratch_shapes=[*sems(7 * count), pltpu.SemaphoreType.DMA((count,))],
        compiler_params=params(ident),
    )(*arrays)


def group_reduce_kernel(count, *refs):
    ps, os = refs[:count], refs[count : 2 * count]
    cb, sb, rb, nb, rn, send_sems, recv_sems = refs[2 * count :]
    me = here()
    y, c = me["y"], me["c"]
    partner, other = at(me, c=1), at(me, n=1)
    ys = {d: at(me, y=d) for d in (1, 2, 3)}
    greet([partner, other, *ys.values()])
    copies = Copies(send_sems, recv_sems)
    cores, sent = {}, {}
    for i in range(count):
        for d in (2, 1, 3, 0):
            yi = step(me, "y", d)
            cores[i, d] = copies.send(ps[i].at[yi, 1 - c], cb.at[i, d], partner)
    for i in range(count):
        for d in (2, 1, 3):
            cores[i, d].wait_recv()
            sb[i, d - 1] = (ps[i][step(me, "y", d), c].astype(f32) + cb[i, d].astype(f32)).astype(bf16)
            sent[i, d] = copies.send(sb.at[i, d - 1], rb.at[i, d - 1], ys[d])
    last = []
    for i in range(count):
        cores[i, 0].wait_recv()
        total = ps[i][y, c].astype(f32) + cb[i, 0].astype(f32)
        for d in (1, 3, 2):
            sent[i, d].wait_recv()
            total = total + rb[i, d - 1].astype(f32)
        nb[i] = total.astype(bf16)
        last.append(copies.send(nb.at[i], rn.at[i], other))
    for i in range(count):
        last[i].wait_recv()
        os[i][...] = nb[i].astype(f32) + rn[i].astype(f32)
    copies.finish()


def group_reduce(ident, arrays):
    count = len(arrays)
    return pl.pallas_call(
        functools.partial(group_reduce_kernel, count),
        out_shape=[jax.ShapeDtypeStruct((TOK, D), f32) for _ in arrays],
        in_specs=[VMEM] * count,
        out_specs=[VMEM] * count,
        scratch_shapes=[
            pltpu.VMEM((count, 4, TOK, D), bf16),
            pltpu.VMEM((count, 3, TOK, D), bf16),
            pltpu.VMEM((count, 3, TOK, D), bf16),
            pltpu.VMEM((count, TOK, D), bf16),
            pltpu.VMEM((count, TOK, D), bf16),
            *sems(8 * count),
        ],
        compiler_params=params(ident),
    )(*arrays)


def narrow_sum_kernel(x, o, rn, send_sems, recv_sems):
    me = here()
    other = at(me, n=1)
    greet([other])
    copies = Copies(send_sems, recv_sems)
    copies.send(x, rn, other).wait_recv()
    o[...] = x[...].astype(f32) + rn[...].astype(f32)
    copies.finish()


def narrow_sum(ident, array):
    return pl.pallas_call(
        narrow_sum_kernel,
        out_shape=jax.ShapeDtypeStruct(array.shape, f32),
        in_specs=[VMEM],
        out_specs=VMEM,
        scratch_shapes=[pltpu.VMEM(array.shape, bf16), *sems(1)],
        compiler_params=params(ident),
    )(array)


def weight_reduce_kernel(count, *refs):
    ps, small = refs[:count], refs[count]
    os, small_out = refs[count + 1 : 2 * count + 1], refs[2 * count + 1]
    scratch = refs[2 * count + 2 :]
    r1, s1, r2, t2, r3 = (scratch[k * count : (k + 1) * count] for k in range(5))
    e1, e2, e3, f1, f2, send_sems, recv_sems = scratch[5 * count :]
    me = here()
    z, y, xh, c = me["z"], me["y"], me["xh"], me["c"]
    partner = at(me, c=1)
    zs = {d: at(me, z=d) for d in (1, 2, 3)}
    moves = [(d, e) for d in (1, 3, 2, 0) for e in (0, 1) if d or e]
    near = {m: at(me, y=m[0], xh=m[1]) for m in moves}
    greet([partner, *zs.values(), *near.values()])
    copies = Copies(send_sems, recv_sems)
    first, first_small = {}, {}
    for d in (1, 3, 2):
        first_small[d] = copies.send(small, e1.at[d - 1], zs[d])
    for i in range(count):
        for d in (1, 3, 2):
            first[i, d] = copies.send(ps[i].at[step(me, "z", d)], r1[i].at[d - 1], zs[d])
    for d in (1, 3, 2):
        first_small[d].wait_recv()
    f1[...] = small[...] + e1[0] + e1[1] + e1[2]
    second_small = {m: copies.send(f1, e2.at[k], near[m]) for k, m in enumerate(moves)}
    second = {}
    for i in range(count):
        for d in (1, 3, 2):
            first[i, d].wait_recv()
        for yi in range(4):
            for xi in range(2):
                rows = pl.ds(96 * yi + 48 * xi, 48)
                total = ps[i][z, rows].astype(f32)
                for d in range(3):
                    total = total + r1[i][d, rows].astype(f32)
                s1[i][yi, xi] = total.astype(bf16)
        for m in moves:
            second[i, m] = copies.send(
                s1[i].at[step(me, "y", m[0]), step(me, "xh", m[1])], r2[i].at[y, xh], near[m]
            )
        r2[i][y, xh] = s1[i][y, xh]
    for m in moves:
        second_small[m].wait_recv()
    f2[...] = f1[...]
    for k in range(len(moves)):
        f2[...] = f2[...] + e2[k]
    third_small = copies.send(f2, e3, partner)
    third = []
    keep, give = pl.ds(pl.multiple_of(24 * c, 8), 24), pl.ds(pl.multiple_of(24 * (1 - c), 8), 24)
    for i in range(count):
        for m in moves:
            second[i, m].wait_recv()
        t2[i][...] = r2[i][:, 0].astype(f32) + r2[i][:, 1].astype(f32)
        third.append(copies.send(t2[i].at[:, give], r3[i], partner))
        os[i][:, c] = t2[i][:, keep]
    for i in range(count):
        third[i].wait_recv()
        os[i][:, 1 - c] = r3[i][...]
    third_small.wait_recv()
    small_out[...] = f2[...] + e3[...]
    copies.finish()


def weight_reduce(ident, arrays, small):
    count = len(arrays)
    cols = [a.shape[-1] for a in arrays]
    rows = small.shape[0]
    return pl.pallas_call(
        functools.partial(weight_reduce_kernel, count),
        out_shape=[jax.ShapeDtypeStruct((4, 2, 24, n), f32) for n in cols]
        + [jax.ShapeDtypeStruct(small.shape, f32)],
        in_specs=[VMEM] * (count + 1),
        out_specs=[VMEM] * (count + 1),
        scratch_shapes=[
            *[pltpu.VMEM((3, 384, n), bf16) for n in cols],
            *[pltpu.VMEM((4, 2, 48, n), bf16) for n in cols],
            *[pltpu.VMEM((4, 2, 48, n), bf16) for n in cols],
            *[pltpu.VMEM((4, 48, n), f32) for n in cols],
            *[pltpu.VMEM((4, 24, n), f32) for n in cols],
            pltpu.VMEM((3, rows, D), f32),
            pltpu.VMEM((7, rows, D), f32),
            pltpu.VMEM((rows, D), f32),
            pltpu.VMEM((rows, D), f32),
            pltpu.VMEM((rows, D), f32),
            *sems(11 * (count + 1)),
        ],
        compiler_params=params(ident),
    )(*arrays, small)


def heads_in(ref, scratch):
    for h in range(HEADS):
        scratch[pl.ds(h * TOK, TOK), :] = ref[:, pl.ds(h * HD, HD)]


def attend_kernel(q_in, kv, start, ids, o, exact, lse, q, top, total, acc, low_acc):
    me = here()
    shard = ((me["z"] * 4 + me["y"]) * 2 + me["xh"]) * 2 + me["c"]
    last = shard // BLOCK_SHARDS
    heads_in(q_in, q)
    top[...] = jnp.full_like(top, big_negative)
    total[...] = jnp.zeros_like(total)
    acc[...] = jnp.zeros_like(acc)
    low_acc[...] = jnp.zeros_like(low_acc)

    def block(index, masked):
        offset = pl.multiple_of(index * KEY_BLOCK, KEY_BLOCK)
        rows = pl.ds(offset, KEY_BLOCK)
        keys = kv[rows, pl.ds(0, HD)]
        values = kv[rows, pl.ds(HD, HD)].T
        for chunk in range(NQ // Q_CHUNK):
            cs = pl.ds(chunk * Q_CHUNK, Q_CHUNK)
            scores = nt(keys, q[cs, :]) * SCALE_LOG2
            if masked:
                key_ids = offset + lax.broadcasted_iota(jnp.int32, (KEY_BLOCK, Q_CHUNK), 0)
                allowed = (key_ids >= start[:, cs]) & (key_ids <= ids[:, cs])
                scores = jnp.where(allowed, scores, big_negative)
            old = top[:, cs]
            new = jnp.maximum(old, jnp.max(scores, axis=0, keepdims=True))
            probs = jnp.exp2(scores - new)
            if masked:
                probs = jnp.where(allowed, probs, 0.0)
            fade = jnp.exp2(old - new)
            top[:, cs] = new
            total[:, cs] = total[:, cs] * fade + jnp.sum(probs, axis=0, keepdims=True)
            high = probs.astype(bf16)
            rest = (probs - high.astype(f32)).astype(bf16)
            acc[:, cs] = acc[:, cs] * fade + nn(values, high)
            low_acc[:, cs] = low_acc[:, cs] * fade + nn(values, rest)

    @pl.when(last > 0)
    def _():
        block(0, True)

        @pl.loop(1, last)
        def _(index):
            block(index, False)

        kept = start[...] < last * KEY_BLOCK
        top[...] = jnp.where(kept, top[...], big_negative)
        kept = kept.astype(f32)
        total[...] = total[...] * kept
        acc[...] = acc[...] * kept
        low_acc[...] = low_acc[...] * kept

    block(last, True)
    inverse = 1.0 / total[...]
    rows = acc[...] * inverse
    exact[...] = rows + low_acc[...] * inverse
    rows = rows.T.astype(bf16)
    for h in range(HEADS):
        o[:, pl.ds(h * HD, HD)] = rows[h * TOK : (h + 1) * TOK]
    lse[...] = top[...] + jnp.log2(total[...])


def attend(queries, kv, start, ids):
    return pl.pallas_call(
        attend_kernel,
        out_shape=(
            jax.ShapeDtypeStruct((TOK, HEADS * HD), bf16),
            jax.ShapeDtypeStruct((HD, NQ), f32),
            jax.ShapeDtypeStruct((1, NQ), f32),
        ),
        in_specs=[VMEM] * 4,
        out_specs=(VMEM,) * 3,
        scratch_shapes=[
            pltpu.VMEM((NQ, HD), bf16),
            pltpu.VMEM((1, NQ), f32),
            pltpu.VMEM((1, NQ), f32),
            pltpu.VMEM((HD, NQ), f32),
            pltpu.VMEM((HD, NQ), f32),
        ],
        compiler_params=pltpu.CompilerParams(vmem_limit_bytes=60 * 2**20),
    )(queries, kv, start, ids)


def attend_back_kernel(q_in, kv, g_in, exact, start, ids, lse, dq, dkv, q, g, acc):
    me = here()
    shard = ((me["z"] * 4 + me["y"]) * 2 + me["xh"]) * 2 + me["c"]
    last = shard // BLOCK_SHARDS
    heads_in(q_in, q)
    heads_in(g_in, g)
    balance = jnp.sum(g[...].astype(f32).T * exact[...], axis=0, keepdims=True)
    acc[...] = jnp.zeros_like(acc)
    total = lse[...]
    earlier = jnp.where(start[...] < last * KEY_BLOCK, total, -big_negative)

    def block(index, masked, shift):
        offset = pl.multiple_of(index * KEY_BLOCK, KEY_BLOCK)
        rows = pl.ds(offset, KEY_BLOCK)
        keys, values = kv[rows, pl.ds(0, HD)], kv[rows, pl.ds(HD, HD)]
        keys_t = keys.T
        dk = jnp.zeros((KEY_BLOCK, HD), f32)
        dv = jnp.zeros((KEY_BLOCK, HD), f32)
        for chunk in range(NQ // Q_CHUNK):
            cs = pl.ds(chunk * Q_CHUNK, Q_CHUNK)
            part = slice(chunk * Q_CHUNK, (chunk + 1) * Q_CHUNK)
            qc, gc = q[cs, :], g[cs, :]
            probs = jnp.exp2(nt(keys, qc) * SCALE_LOG2 - shift[:, part])
            if masked:
                key_ids = offset + lax.broadcasted_iota(jnp.int32, (KEY_BLOCK, Q_CHUNK), 0)
                allowed = (key_ids >= start[:, cs]) & (key_ids <= ids[:, cs])
                probs = jnp.where(allowed, probs, 0.0)
            grads = (probs * (nt(values, gc) - balance[:, part])).astype(bf16)
            dv = dv + nn(probs.astype(bf16), gc)
            dk = dk + nn(grads, qc)
            acc[:, cs] = acc[:, cs] + nn(keys_t, grads)
        dkv[rows, pl.ds(0, HD)] = (dk * SCALE).astype(bf16)
        dkv[rows, pl.ds(HD, HD)] = dv.astype(bf16)

    @pl.when(last > 0)
    def _():
        block(0, True, earlier)

        @pl.loop(1, last)
        def _(index):
            block(index, False, earlier)

    block(last, True, total)

    @pl.loop(last + 1, TOKENS // KEY_BLOCK)
    def _(index):
        dkv[pl.ds(pl.multiple_of(index * KEY_BLOCK, KEY_BLOCK), KEY_BLOCK), :] = jnp.zeros(
            (KEY_BLOCK, 2 * HD), bf16
        )

    rows = (acc[...] * SCALE).T
    for h in range(HEADS):
        dq[:, pl.ds(h * HD, HD)] = rows[h * TOK : (h + 1) * TOK]


def attend_back(queries, kv, grads, exact, start, ids, lse):
    return pl.pallas_call(
        attend_back_kernel,
        out_shape=(
            jax.ShapeDtypeStruct((TOK, HEADS * HD), f32),
            jax.ShapeDtypeStruct((TOKENS, 2 * HD), bf16),
        ),
        in_specs=[VMEM] * 7,
        out_specs=(VMEM,) * 2,
        scratch_shapes=[
            pltpu.VMEM((NQ, HD), bf16),
            pltpu.VMEM((NQ, HD), bf16),
            pltpu.VMEM((HD, NQ), f32),
        ],
        compiler_params=pltpu.CompilerParams(vmem_limit_bytes=60 * 2**20),
    )(queries, kv, grads, exact, start, ids, lse)


def row_starts(lengths, token_ids):
    ends = jnp.cumsum(lengths)
    before = ends[None, :] <= token_ids[:, None]
    return jnp.sum(jnp.where(before, lengths[None, :], 0), axis=1)


def rope_tables(positions):
    half = HD // 2
    freqs = rope_base ** (-2.0 * jnp.arange(half, dtype=f32) / HD)
    angles = positions.astype(f32)[:, None] * freqs[None, :]
    cosine, sine = jnp.cos(angles), jnp.sin(angles)
    return jnp.concatenate([cosine, cosine], 1), jnp.concatenate([-sine, sine], 1)


def rotate(values, cosine, sine):
    heads = []
    for h in range(values.shape[1] // HD):
        one = values[:, h * HD : (h + 1) * HD]
        swapped = jnp.concatenate([one[:, HD // 2 :], one[:, : HD // 2]], axis=1)
        heads.append(one * cosine + swapped * sine)
    return jnp.concatenate(heads, axis=1)


def normalize(values):
    inverse = lax.rsqrt(jnp.mean(values * values, axis=-1) + rms_eps)
    return (values * inverse[:, None], inverse)


def norm_back(grad_normed, normed, inverse):
    inner = jnp.mean(grad_normed * normed, axis=-1, keepdims=True)
    return inverse[:, None] * (grad_normed - normed * inner)


def shards(
    layer_in, lengths, norm_attn, w_qkv, qkv_bias, w_out, norm_mlp, w_gate, w_up, w_down, out_grad
):
    shard = lax.axis_index(WIDE)
    member = lax.axis_index(("y", "c"))
    own_ids = shard * TOK + jnp.arange(TOK, dtype=jnp.int32)
    seq_starts = row_starts(lengths, own_ids)
    cosine, sine = rope_tables(own_ids - seq_starts)
    start = jnp.tile(seq_starts, HEADS)[None]
    ids = jnp.tile(own_ids, HEADS)[None]
    gate_w = lax.dynamic_slice(w_gate, (0, member * UNITS), (D, UNITS))
    up_w = lax.dynamic_slice(w_up, (0, member * UNITS), (D, UNITS))
    down_w = lax.dynamic_slice(w_down, (member * UNITS, 0), (UNITS, D))

    input_f32 = layer_in.astype(f32)
    normed_attn, inverse_attn = normalize(input_f32)
    act_attn = (normed_attn * norm_attn).astype(bf16)
    projected = nn(act_attn, w_qkv) + qkv_bias[0]
    turned = rotate(projected[:, : (HEADS + 1) * HD], cosine, sine).astype(bf16)
    queries = turned[:, : HEADS * HD]
    kv_own = jnp.concatenate(
        [turned[:, HEADS * HD :], projected[:, (HEADS + 1) * HD :].astype(bf16)], axis=1
    )
    kv = kv_gather(kv_own).reshape(TOKENS, 2 * HD)
    attn_low, exact, lse = attend(queries, kv, start, ids)

    resid = input_f32 + narrow_sum(3, nn(attn_low, w_out).astype(bf16))
    normed_mlp, inverse_mlp = normalize(resid)
    act_mlp = (normed_mlp * norm_mlp).astype(bf16)
    act_all, out_grad_all = (
        a.reshape(GROUP * TOK, D) for a in group_gather(4, [act_mlp, out_grad])
    )
    gate = nn(act_all, gate_w)
    up = nn(act_all, up_w)
    sigmoid = jax.nn.sigmoid(gate)
    silu = gate * sigmoid
    hidden = (silu * up).astype(bf16)
    grad_hidden = nt(out_grad_all, down_w)
    grad_gate_pre = (grad_hidden * up * (sigmoid * (1.0 + gate * (1.0 - sigmoid)))).astype(bf16)
    grad_up_pre = (grad_hidden * silu).astype(bf16)
    down_terms = nn(hidden, down_w).astype(bf16).reshape(4, 2, TOK, D)
    back_terms = (nt(grad_gate_pre, gate_w) + nt(grad_up_pre, up_w)).astype(bf16)
    mlp_out, grad_act_mlp = group_reduce(5, [down_terms, back_terms.reshape(4, 2, TOK, D)])
    layer_out = (resid + mlp_out).astype(bf16)
    grad_norm_mlp = jnp.sum(grad_act_mlp * normed_mlp, axis=0)
    grad_resid = out_grad.astype(f32) + norm_back(
        grad_act_mlp * norm_mlp, normed_mlp, inverse_mlp
    )
    grad_branch = grad_resid.astype(bf16)
    grad_attn = nt(grad_branch, w_out).astype(bf16)
    grad_q, grad_kv_terms = attend_back(queries, kv, grad_attn, exact, start, ids, lse)
    grad_kv = kv_reduce(grad_kv_terms.reshape(4, 4, 2, 2, TOK, 2 * HD))
    grad_turned = jnp.concatenate([grad_q, grad_kv[:, :HD]], axis=1)
    grad_projected = jnp.concatenate(
        [rotate(grad_turned, cosine, -sine), grad_kv[:, HD:]], axis=1
    ).astype(bf16)
    grad_act_attn = narrow_sum(6, nt(grad_projected, w_qkv).astype(bf16))
    grad_norm_attn = jnp.sum(grad_act_attn * normed_attn, axis=0)
    in_grad = (
        grad_resid + norm_back(grad_act_attn * norm_attn, normed_attn, inverse_attn)
    ).astype(bf16)

    act_attn_all, branch_all = (
        a.reshape(GROUP * TOK, D) for a in group_gather(7, [act_attn, grad_branch])
    )
    by_head = grad_projected.reshape(TOK, 4, 2, HD).transpose(1, 2, 0, 3)
    low_cols = attn_low.reshape(TOK, 4, 2, OUT_COLS).transpose(1, 2, 0, 3)
    head_grads, low_all = (
        a.reshape(GROUP * TOK, -1) for a in group_swap(8, [by_head, low_cols])
    )
    bias_sums = jnp.sum(grad_projected.astype(f32), axis=0)
    small = jnp.concatenate(
        [
            grad_norm_attn[None],
            grad_norm_mlp[None],
            jnp.pad(bias_sums, (0, D - bias_sums.shape[0]))[None],
            jnp.zeros((5, D), f32),
        ]
    )
    terms = [
        tn(act_all, grad_gate_pre),
        tn(act_all, grad_up_pre),
        tn(out_grad_all, hidden),
        tn(act_attn_all, head_grads),
        tn(branch_all, low_all),
    ]
    *sums, small = weight_reduce(
        9, [t.astype(bf16).reshape(4, D // 4, t.shape[1]) for t in terms], small
    )
    sum_gate, sum_up, sum_down, sum_qkv, sum_out = (
        s.transpose(2, 0, 1, 3).reshape(24, -1) for s in sums
    )
    norms = lax.dynamic_slice(small, (0, shard * 24), (2, 24))
    bias = lax.dynamic_slice(
        small[2, : (HEADS + 2) * HD].reshape(HEADS + 2, HD), (0, shard * 2), (HEADS + 2, 2)
    )
    return (
        layer_out,
        in_grad,
        norms[0],
        sum_qkv,
        bias[None, : HEADS + 1],
        bias[HEADS + 1 :],
        sum_out.T,
        norms[1],
        sum_gate,
        sum_up,
        sum_down.T,
    )


def solution(mesh):
    torus = Mesh(mesh.devices.reshape(4, 4, 2, 2, 2), AXES)
    in_specs = (
        P(WIDE, None),
        P(),
        P(),
        P(None, "n"),
        P("n", None),
        P("n", None),
        P(),
        P(None, "n"),
        P(None, "n"),
        P("n", None),
        P(WIDE, None),
    )
    out_specs = (
        P(WIDE, None),
        P(WIDE, None),
        P(WIDE),
        P(WIDE, "n"),
        P("n", None, WIDE),
        P("n", WIDE),
        P("n", WIDE),
        P(WIDE),
        P(WIDE, "n"),
        P(WIDE, "n"),
        P("n", WIDE),
    )
    return jax.shard_map(
        shards, mesh=torus, in_specs=in_specs, out_specs=out_specs, check_vma=False
    )
```

time: 1470 us -> 514 us (0.35)
  waiting for transfers between devices: 576 us -> 0 us
  Pallas kernels: 0 us -> 372 us
  blocking collectives: 362 us -> 0 us
  starting transfers between devices: 278 us -> 0 us
  matrix products: 126 us -> 61.4 us
  other arithmetic: 40.9 us -> 21.9 us
    unnamed x8 -> x0, waiting for transfers between devices: 505 us -> none
    pallas_call x0 -> x11, Pallas kernels: none -> 372 us  [the longest x1 90 us: weight_reduce(): pl.pallas_call(functools.partial(weight_reduce_kernel, count), out_shape=...]
    unnamed x1 -> x0, blocking collectives: 325 us -> none
    all_to_all x5 -> x0, starting transfers between devices: 278 us -> none  [the longest x1 253 us: sum_by_axis(): return jnp.sum(lax.all_to_all(own, far, 0, 0, tiled=True), axis=0)]
    all_to_all x5 -> x0, waiting for transfers between devices: 71.1 us -> none  [the longest x1 49.5 us: sum_by_axis(): return jnp.sum(lax.all_to_all(own, far, 0, 0, tiled=True), axis=0)]
    dot_general x24 -> x15, matrix products: 126 us -> 61.4 us  [the longest x5 21 us: tn(): lax.dot_general(a, b, (((0,), (0,)), ((), ())), preferred_element_type=f32)]
    all_to_all x3 -> x0, blocking collectives: 36.9 us -> none  [the longest x2 22.4 us: copy_for_each(): lax.all_to_all(jnp.broadcast_to(array[None], (peers, *array.shape)), axis...]
    convert_element_type x0 -> x6, local copies, waits for them, and re-layouts: none -> 17.4 us  [the longest x4 13.8 us: shards(): t.astype(bf16).reshape(4, D // 4, t.shape[1])]
  transfers between devices with their start and end apart: 10 -> 0, of which waited for: 8 -> 0; matrix products, arithmetic and copies ran while one was open for 10% -> 0% of each run, Pallas kernels for 0% -> 0%
where the time goes in v1:
time: 514 us; the launch traced here: 509 us
  Pallas kernels  372 us (72%)
  matrix products  61.4 us (12%)
  local copies, waits for them, and re-layouts  51.9 us (10%)
  other arithmetic  21.9 us (4%)
    pallas_call x1, Pallas kernels, weight_reduce(): pl.pallas_call(functools.partial(weight_reduce_kernel, count), out_shape=...  90 us
    pallas_call x2, Pallas kernels, group_gather(): pl.pallas_call(functools.partial(group_gather_kernel, count), out_shape=[...  83.5 us
    pallas_call x1, Pallas kernels, kv_reduce(): pl.pallas_call(kv_reduce_kernel, out_shape=jax.ShapeDtypeStruct((TOK, wid...  62.7 us
    pallas_call x1, Pallas kernels, group_reduce(): pl.pallas_call(functools.partial(group_reduce_kernel, count), out_shape=[...  53.9 us
    pallas_call x1, Pallas kernels, kv_gather(): pl.pallas_call(kv_gather_kernel, out_shape=jax.ShapeDtypeStruct((4, 4, 2,...  33.1 us
    pallas_call x2, Pallas kernels, narrow_sum(): pl.pallas_call(narrow_sum_kernel, out_shape=jax.ShapeDtypeStruct(array.sh...  23.6 us
    dot_general x5, matrix products, tn(): lax.dot_general(a, b, (((0,), (0,)), ((), ())), preferred_element_type=f32)  21 us
    dot_general x5, matrix products, nt(): lax.dot_general(a, b, (((1,), (1,)), ((), ())), preferred_element_type=f32)  20.7 us

profile of v1, /device:TPU:1, one launch (start us, length us, event | category | flops | bytes accessed | tf_op | source)
XLA Modules:
  0.0 508.6 jit_solution(7688558821881642927)
XLA Ops:
  8.0 33.1 %shard_map.194 = bf16[4,4,2,2,128,256]{5,4,3,2,1,0:T(8,128)(2,1)} custom-call(bf16[128,256]{1,0:T(8,128)(2,1)} %pad_maximum_fusion.2.x), custom_call_target="tpu_custom_call" | custom-call | tf_op jit(solution)/shard_map/pallas_call | solution.py:164
  41.8 5.0 shard_map.195
  49.8 12.7 %shard_map.196 = f32[128,1536]{1,0:T(8,128)} custom-call(bf16[128,1536]{1,0:T(8,128)(2,1)} %convolution_convert_fusion.5.x), custom_call_target="tpu_custom_call" | custom-call | tf_op jit(solution)/shard_map/pallas_call | solution.py:383
  65.6 42.9 %shard_map.197 = (bf16[4,2,128,1536]{3,2,1,0:T(8,128)(2,1)}, bf16[4,2,128,1536]{3,2,1,0:T(8,128)(2,1)}) custom-call(bf16[128,1536]{1,0:T(8,128)(2,1)} %multiply_convert_fusion.3.refs_0_, bf16[128,1536]{1,0:T(8,128)(2,1)} %refs_1_.1), custom_call_target="tpu_custom_call" | custom-call | tf_op jit(solution)/shard_map/pallas_call | solution.py:277
  108.5 5.4 %fusion.4 = f32[1024,560]{0,1:T(8,128)S(1)} fusion(bf16[1024,1536]{1,0:T(8,128)(2,1)} %bitcast.105, bf16[1536,4480]{1,0:T(8,128)(2,1)} %param.19, s32[]{:T(128)S(6)} %select_n.16), kind=kOutput, calls=%fused_computation.17 | convolution fusion | flops 1761607680 | bytes 7405572 | tf_op jit(solution)/shard_map/dot_general | solution.py:47
  113.9 4.4 fusion.8
  118.3 4.2 multiply_convert_fusion
  122.5 6.2 %fusion.6 = f32[1024,1536]{1,0:T(8,128)S(1)} fusion(bf16[1024,560]{0,1:T(8,128)(2,1)S(1)} %get-tuple-element.58, bf16[1536,4480]{1,0:T(8,128)(2,1)} %param.18, s32[]{:T(128)S(6)} %select_n.16), kind=kOutput, calls=%fused_computation.19 | convolution fusion | flops 1761607680 | bytes 9404420 | tf_op jit(solution)/shard_map/dot_general | solution.py:51
  128.8 6.9 %add_convert_fusion = bf16[1024,1536]{1,0:T(8,128)(2,1)} fusion(f32[1024,1536]{1,0:T(8,128)S(1)} %fusion.6, bf16[1024,560]{0,1:T(8,128)(2,1)S(1)} %get-tuple-element.57, bf16[1536,4480]{1,0:T(8,128)(2,1)} %param.19, s32[]{:T(128)S(6)} %select_n.16), kind=kOutput, calls=%fused_computation | convolution fusion | flops 1764753408 | bytes 12550148 | tf_op jit(solution)/shard_map/dot_general | solution.py:51
  135.7 5.5 %convolution_convert_fusion = bf16[1024,1536]{1,0:T(8,128)(2,1)} fusion(bf16[1024,560]{0,1:T(8,128)(2,1)S(1)} %get-tuple-element.59, bf16[4480,1536]{1,0:T(8,128)(2,1)} %param.20, s32[]{:T(128)S(6)} %select_n.16), kind=kOutput, calls=%fused_computation.1 | convolution fusion | flops 1763180544 | bytes 6012932 | tf_op jit(solution)/shard_map/dot_general | solution.py:47
  141.1 53.9 %shard_map.198 = (f32[128,1536]{1,0:T(8,128)}, f32[128,1536]{1,0:T(8,128)}) custom-call(bf16[4,2,128,1536]{3,2,1,0:T(8,128)(2,1)} %bitcast.85, bf16[4,2,128,1536]{3,2,1,0:T(8,128)(2,1)} %bitcast.84), custom_call_target="tpu_custom_call" | custom-call | tf_op jit(solution)/shard_map/pallas_call | solution.py:355
  200.3 6.5 %shard_map.199 = (f32[128,768]{1,0:T(8,128)}, bf16[8192,256]{1,0:T(8,128)(2,1)}) custom-call(bf16[128,768]{1,0:T(8,128)(2,1)} %copy-done.10, bf16[8192,256]{1,0:T(8,128)(2,1)} %bitcast.79, bf16[128,768]{1,0:T(8,128)(2,1)} %convolution_convert_fusion.6.g_in, f32[128,768]{1,0:T(8,128)} %get-tuple-element.35.exact, s32[1,768]{1,0:T(1,128)} %get-tuple-element.112.start, ...), custom_call_target="tpu_custom_call" | custom-call | tf_op jit(solution)/shard_map/pallas_call | solution.py:624
  210.6 62.7 %shard_map.200 = f32[128,256]{1,0:T(8,128)} custom-call(bf16[4,4,2,2,128,256]{5,4,3,2,1,0:T(8,128)(2,1)} %bitcast.83), custom_call_target="tpu_custom_call" | custom-call | tf_op jit(solution)/shard_map/pallas_call | solution.py:226
  278.1 10.9 %shard_map.201 = f32[128,1536]{1,0:T(8,128)} custom-call(bf16[128,1536]{1,0:T(8,128)(2,1)} %convolution_convert_fusion.4.x), custom_call_target="tpu_custom_call" | custom-call | tf_op jit(solution)/shard_map/pallas_call | solution.py:383
  299.1 13.8 %shard_map.203 = (bf16[4,2,128,128]{3,2,1,0:T(8,128)(2,1)}, bf16[4,2,128,96]{3,2,1,0:T(8,128)(2,1)}) custom-call(bf16[4,2,128,128]{3,2,1,0:T(8,128)(2,1)} %bitcast.89, bf16[4,2,128,96]{3,2,1,0:T(8,128)(2,1)} %bitcast.88), custom_call_target="tpu_custom_call" | custom-call | tf_op jit(solution)/shard_map/pallas_call | solution.py:309
  312.8 40.6 %shard_map.202 = (bf16[4,2,128,1536]{3,2,1,0:T(8,128)(2,1)}, bf16[4,2,128,1536]{3,2,1,0:T(8,128)(2,1)}) custom-call(bf16[128,1536]{1,0:T(8,128)(2,1)} %copy-done.7, bf16[128,1536]{1,0:T(8,128)(2,1)} %copy-done.8), custom_call_target="tpu_custom_call" | custom-call | tf_op jit(solution)/shard_map/pallas_call | solution.py:277
  353.5 3.3 fusion.1
  358.7 3.8 fusion
  365.6 4.1 copy.46
  369.8 5.4 %convolution_convert_fusion.1 = bf16[1536,560]{0,1:T(8,128)(2,1)} fusion(bf16[1024,560]{0,1:T(8,128)(2,1)} %copy-done.24, bf16[1024,1536]{1,0:T(8,128)(2,1)} %bitcast.109), kind=kOutput, calls=%fused_computation.2 | convolution fusion | flops 1762467840 | bytes 6012928 | tf_op jit(solution)/shard_map/dot_general | solution.py:55
  375.2 3.9 copy.47
  379.1 5.4 %convolution_convert_fusion.3 = bf16[1536,560]{0,1:T(8,128)(2,1)} fusion(bf16[1024,560]{0,1:T(8,128)(2,1)} %copy-done.21, bf16[1024,1536]{1,0:T(8,128)(2,1)} %bitcast.106), kind=kOutput, calls=%fused_computation.4 | convolution fusion | flops 1762467840 | bytes 6012928 | tf_op jit(solution)/shard_map/dot_general | solution.py:55
  384.4 3.9 copy.45
  388.3 90.0 %shard_map.204 = (f32[4,2,24,560]{3,2,1,0:T(8,128)}, f32[4,2,24,560]{3,2,1,0:T(8,128)}, f32[4,2,24,560]{3,2,1,0:T(8,128)}, f32[4,2,24,128]{3,2,1,0:T(8,128)}, f3...) custom-call(bf16[4,384,560]{2,1,0:T(8,128)(2,1)} %bitcast.82, bf16[4,384,560]{2,1,0:T(8,128)(2,1)} %bitcast.80, ...), custom_call_target="tpu_custom_call" | custom-call | tf_op jit(solution)/shard_map/pallas_call | solution.py:459
  (123 shorter events, 72.8 us)
Async XLA Ops:
  0.6 4.1 copy-start
  3.6 1.2 copy-start.15
  4.8 1.7 copy-start.7
  7.3 34.4 %copy-start.10 = (bf16[128,768]{1,0:T(8,128)(2,1)}, bf16[128,768]{1,0:T(8,128)(2,1)S(1)}, u32[]{:S(2)}) copy-start(bf16[128,768]{1,0:T(8,128)(2,1)S(1)} %get-tuple-element.63.q_in) | copy-start | bytes 589828
  46.8 15.8 %copy-start.3 = (bf16[128,1536]{1,0:T(8,128)(2,1)S(1)}, bf16[128,1536]{1,0:T(8,128)(2,1)}, u32[]{:S(2)}) copy-start(bf16[128,1536]{1,0:T(8,128)(2,1)} %param.11) | copy-start | bytes 1179652
  46.8 18.0 %copy-start.11 = (f32[1536]{0:T(1024)S(1)}, f32[1536]{0:T(1024)}, u32[]{:S(2)}) copy-start(f32[1536]{0:T(1024)} %param.17) | copy-start | bytes 18436
  63.9 133.3 %copy-start.14 = (f32[128]{0:T(128)}, f32[128]{0:T(128)S(1)}, u32[]{:S(2)}) copy-start(f32[128]{0:T(128)S(1)} %add_rsqrt_fusion) | copy-start | bytes 1540
  108.5 5.4 %copy-start.18 = (bf16[4,2,128,1536]{3,2,1,0:T(8,128)(2,1)S(1)}, bf16[4,2,128,1536]{3,2,1,0:T(8,128)(2,1)}, u32[]{:S(2)}) copy-start(bf16[4,2,128,1536]{3,2,1,0:T(8,128)(2,1)} %get-tuple-element.31) | copy-start | bytes 9437188
  113.9 4.4 copy-start.20
  122.5 6.2 %copy-start.21 = (bf16[1024,560]{0,1:T(8,128)(2,1)}, bf16[1024,560]{0,1:T(8,128)(2,1)S(1)}, u32[]{:S(2)}) copy-start(bf16[1024,560]{0,1:T(8,128)(2,1)S(1)} %get-tuple-element.58) | copy-start | bytes 3440644
  122.5 6.2 %copy-start.22 = (bf16[1024,560]{0,1:T(8,128)(2,1)}, bf16[1024,560]{0,1:T(8,128)(2,1)S(1)}, u32[]{:S(2)}) copy-start(bf16[1024,560]{0,1:T(8,128)(2,1)S(1)} %get-tuple-element.57) | copy-start | bytes 3440644
  122.5 13.1 %copy-start.24 = (bf16[1024,560]{0,1:T(8,128)(2,1)}, bf16[1024,560]{0,1:T(8,128)(2,1)S(1)}, u32[]{:S(2)}) copy-start(bf16[1024,560]{0,1:T(8,128)(2,1)S(1)} %get-tuple-element.59) | copy-start | bytes 3440644
  141.1 53.9 %copy-start.2 = (f32[128,1536]{1,0:T(8,128)S(1)}, f32[128,1536]{1,0:T(8,128)}, u32[]{:S(2)}) copy-start(f32[128,1536]{1,0:T(8,128)} %copy-done.1) | copy-start | bytes 2359300
  195.0 3.7 copy-start.5
  197.2 3.1 copy-start.17
  198.7 1.6 copy-start.8
  206.8 3.3 copy-start.6
  276.1 15.0 %copy-start.9 = (bf16[128,1024]{1,0:T(8,128)(2,1)}, bf16[128,1024]{1,0:T(8,128)(2,1)S(1)}, u32[]{:S(2)}) copy-start(bf16[128,1024]{1,0:T(8,128)(2,1)S(1)} %slice_dynamic-update-slice_fusion) | copy-start | bytes 786436
  276.1 12.9 %copy-start.4 = (bf16[128,1536]{1,0:T(8,128)(2,1)S(1)}, bf16[128,1536]{1,0:T(8,128)(2,1)}, u32[]{:S(2)}) copy-start(bf16[128,1536]{1,0:T(8,128)(2,1)} %param.11) | copy-start | bytes 1179652
  276.1 12.9 %copy-start.12 = (f32[1536]{0:T(1024)S(1)}, f32[1536]{0:T(1024)}, u32[]{:S(2)}) copy-start(f32[1536]{0:T(1024)} %param.13) | copy-start | bytes 18436
  276.1 12.9 %copy-start.16 = (f32[128]{0:T(128)S(1)}, f32[128]{0:T(128)}, u32[]{:S(2)}) copy-start(f32[128]{0:T(128)} %copy-done.15) | copy-start | bytes 1540
  276.1 15.0 %copy-start.13 = (f32[1536]{0:T(1024)S(1)}, f32[1536]{0:T(1024)}, u32[]{:S(2)}) copy-start(f32[1536]{0:T(1024)} %get-tuple-element.49) | copy-start | bytes 18436
  358.7 3.8 copy-start.19
  358.7 3.8 copy-start.23
  (1 other events, 0.9 us)

commit v2 on v1

--- a/solution.py
+++ b/solution.py
@@ -20,7 +20,6 @@
 NQ = HEADS * TOK
 GROUP = 8
 UNITS = FF // 2 // GROUP
-OUT_COLS = HEADS * HD // GROUP
 
 AXES = ("z", "y", "xh", "c", "n")
 SIZE = {"z": 4, "y": 4, "xh": 2, "c": 2, "n": 2}
@@ -169,80 +168,6 @@
         scratch_shapes=sems(80),
         compiler_params=params(1),
     )(kv)
-
-
-def kv_reduce_kernel(p, o, cb, s, r1a, r1b, ta, tb, r2a, r2b, u, r3, send_sems, recv_sems):
-    me = here()
-    z, y, xh, c = me["z"], me["y"], me["xh"], me["c"]
-    partner, across = at(me, c=1), at(me, xh=1)
-    ys = {d: at(me, y=d) for d in (1, 2, 3)}
-    zs = {d: at(me, z=d) for d in (1, 2, 3)}
-    greet([partner, across, *ys.values(), *zs.values()])
-    copies = Copies(send_sems, recv_sems)
-    half = TOK // 2
-    low, high = pl.ds(0, half), pl.ds(half, half)
-    cores = [
-        copies.send(p.at[:, :, :, 1 - c, rows], cb.at[:, :, :, rows], partner)
-        for rows in (low, high)
-    ]
-    first_a, first_b = {}, {}
-    cores[0].wait_recv()
-    for zi in range(4):
-        s[zi, :, :, low] = (p[zi, :, :, c, low].astype(f32) + cb[zi, :, :, low].astype(f32)).astype(bf16)
-    for d in (1, 3, 2):
-        first_a[d] = copies.send(s.at[step(me, "z", d), :, :, low], r1a.at[d - 1], zs[d])
-    cores[1].wait_recv()
-    for zi in range(4):
-        s[zi, :, :, high] = (p[zi, :, :, c, high].astype(f32) + cb[zi, :, :, high].astype(f32)).astype(bf16)
-    for d in (1, 3, 2):
-        first_b[d] = copies.send(s.at[:, step(me, "y", d), :, high], r1b.at[d - 1], ys[d])
-    for d in (1, 3, 2):
-        first_a[d].wait_recv()
-    ta[...] = (s[z, :, :, low].astype(f32) + r1a[0].astype(f32) + r1a[1].astype(f32) + r1a[2].astype(f32)).astype(bf16)
-    second_a, second_b = {}, {}
-    for d in (1, 3, 2):
-        second_a[d] = copies.send(ta.at[step(me, "y", d)], r2a.at[d - 1], ys[d])
-    for d in (1, 3, 2):
-        first_b[d].wait_recv()
-    tb[...] = (s[:, y, :, high].astype(f32) + r1b[0].astype(f32) + r1b[1].astype(f32) + r1b[2].astype(f32)).astype(bf16)
-    for d in (1, 3, 2):
-        second_b[d] = copies.send(tb.at[step(me, "z", d)], r2b.at[d - 1], zs[d])
-    for d in (1, 3, 2):
-        second_a[d].wait_recv()
-        second_b[d].wait_recv()
-    ua = ta[y].astype(f32) + r2a[0].astype(f32) + r2a[1].astype(f32) + r2a[2].astype(f32)
-    ub = tb[z].astype(f32) + r2b[0].astype(f32) + r2b[1].astype(f32) + r2b[2].astype(f32)
-    u[:, low] = ua.astype(bf16)
-    u[:, high] = ub.astype(bf16)
-    last = copies.send(u.at[1 - xh], r3, across)
-    last.wait_recv()
-    o[...] = u[xh].astype(f32) + r3[...].astype(f32)
-    copies.finish()
-
-
-def kv_reduce(terms):
-    half = TOK // 2
-    wide = 2 * HD
-    return pl.pallas_call(
-        kv_reduce_kernel,
-        out_shape=jax.ShapeDtypeStruct((TOK, wide), f32),
-        in_specs=[VMEM],
-        out_specs=VMEM,
-        scratch_shapes=[
-            pltpu.VMEM((4, 4, 2, TOK, wide), bf16),
-            pltpu.VMEM((4, 4, 2, TOK, wide), bf16),
-            pltpu.VMEM((3, 4, 2, half, wide), bf16),
-            pltpu.VMEM((3, 4, 2, half, wide), bf16),
-            pltpu.VMEM((4, 2, half, wide), bf16),
-            pltpu.VMEM((4, 2, half, wide), bf16),
-            pltpu.VMEM((3, 2, half, wide), bf16),
-            pltpu.VMEM((3, 2, half, wide), bf16),
-            pltpu.VMEM((2, TOK, wide), bf16),
-            pltpu.VMEM((TOK, wide), bf16),
-            *sems(16),
-        ],
-        compiler_params=params(2),
-    )(terms)
 
 
 def group_gather_kernel(count, *refs):
@@ -277,38 +202,6 @@
     return pl.pallas_call(
         functools.partial(group_gather_kernel, count),
         out_shape=[jax.ShapeDtypeStruct((4, 2, *a.shape), a.dtype) for a in arrays],
-        in_specs=[ANY] * count,
-        out_specs=[ANY] * count,
-        scratch_shapes=[*sems(7 * count), pltpu.SemaphoreType.DMA((count,))],
-        compiler_params=params(ident),
-    )(*arrays)
-
-
-def group_swap_kernel(count, *refs):
-    xs, os, (send_sems, recv_sems, local_sems) = refs[:count], refs[count : 2 * count], refs[2 * count :]
-    me = here()
-    y, c = me["y"], me["c"]
-    moves = [(d, e) for d in (1, 3, 2, 0) for e in (0, 1) if d or e]
-    greet([at(me, y=d, c=e) for d, e in moves])
-    copies = Copies(send_sems, recv_sems)
-    local = []
-    for i, (x, o) in enumerate(zip(xs, os)):
-        for d, e in moves:
-            copies.send(x.at[step(me, "y", d), step(me, "c", e)], o.at[y, c], at(me, y=d, c=e))
-        local.append(pltpu.make_async_copy(x.at[y, c], o.at[y, c], local_sems.at[i]))
-        local[-1].start()
-    for copy in local:
-        copy.wait()
-    for copy in copies.started:
-        copy.wait_recv()
-    copies.finish()
-
-
-def group_swap(ident, arrays):
-    count = len(arrays)
-    return pl.pallas_call(
-        functools.partial(group_swap_kernel, count),
-        out_shape=[jax.ShapeDtypeStruct(a.shape, a.dtype) for a in arrays],
         in_specs=[ANY] * count,
         out_specs=[ANY] * count,
         scratch_shapes=[*sems(7 * count), pltpu.SemaphoreType.DMA((count,))],
@@ -390,95 +283,6 @@
     )(array)
 
 
-def weight_reduce_kernel(count, *refs):
-    ps, small = refs[:count], refs[count]
-    os, small_out = refs[count + 1 : 2 * count + 1], refs[2 * count + 1]
-    scratch = refs[2 * count + 2 :]
-    r1, s1, r2, t2, r3 = (scratch[k * count : (k + 1) * count] for k in range(5))
-    e1, e2, e3, f1, f2, send_sems, recv_sems = scratch[5 * count :]
-    me = here()
-    z, y, xh, c = me["z"], me["y"], me["xh"], me["c"]
-    partner = at(me, c=1)
-    zs = {d: at(me, z=d) for d in (1, 2, 3)}
-    moves = [(d, e) for d in (1, 3, 2, 0) for e in (0, 1) if d or e]
-    near = {m: at(me, y=m[0], xh=m[1]) for m in moves}
-    greet([partner, *zs.values(), *near.values()])
-    copies = Copies(send_sems, recv_sems)
-    first, first_small = {}, {}
-    for d in (1, 3, 2):
-        first_small[d] = copies.send(small, e1.at[d - 1], zs[d])
-    for i in range(count):
-        for d in (1, 3, 2):
-            first[i, d] = copies.send(ps[i].at[step(me, "z", d)], r1[i].at[d - 1], zs[d])
-    for d in (1, 3, 2):
-        first_small[d].wait_recv()
-    f1[...] = small[...] + e1[0] + e1[1] + e1[2]
-    second_small = {m: copies.send(f1, e2.at[k], near[m]) for k, m in enumerate(moves)}
-    second = {}
-    for i in range(count):
-        for d in (1, 3, 2):
-            first[i, d].wait_recv()
-        for yi in range(4):
-            for xi in range(2):
-                rows = pl.ds(96 * yi + 48 * xi, 48)
-                total = ps[i][z, rows].astype(f32)
-                for d in range(3):
-                    total = total + r1[i][d, rows].astype(f32)
-                s1[i][yi, xi] = total.astype(bf16)
-        for m in moves:
-            second[i, m] = copies.send(
-                s1[i].at[step(me, "y", m[0]), step(me, "xh", m[1])], r2[i].at[y, xh], near[m]
-            )
-        r2[i][y, xh] = s1[i][y, xh]
-    for m in moves:
-        second_small[m].wait_recv()
-    f2[...] = f1[...]
-    for k in range(len(moves)):
-        f2[...] = f2[...] + e2[k]
-    third_small = copies.send(f2, e3, partner)
-    third = []
-    keep, give = pl.ds(pl.multiple_of(24 * c, 8), 24), pl.ds(pl.multiple_of(24 * (1 - c), 8), 24)
-    for i in range(count):
-        for m in moves:
-            second[i, m].wait_recv()
-        t2[i][...] = r2[i][:, 0].astype(f32) + r2[i][:, 1].astype(f32)
-        third.append(copies.send(t2[i].at[:, give], r3[i], partner))
-        os[i][:, c] = t2[i][:, keep]
-    for i in range(count):
-        third[i].wait_recv()
-        os[i][:, 1 - c] = r3[i][...]
-    third_small.wait_recv()
-    small_out[...] = f2[...] + e3[...]
-    copies.finish()
-
-
-def weight_reduce(ident, arrays, small):
-    count = len(arrays)
-    cols = [a.shape[-1] for a in arrays]
-    rows = small.shape[0]
-    return pl.pallas_call(
-        functools.partial(weight_reduce_kernel, count),
-        out_shape=[jax.ShapeDtypeStruct((4, 2, 24, n), f32) for n in cols]
-        + [jax.ShapeDtypeStruct(small.shape, f32)],
-        in_specs=[VMEM] * (count + 1),
-        out_specs=[VMEM] * (count + 1),
-        scratch_shapes=[
-            *[pltpu.VMEM((3, 384, n), bf16) for n in cols],
-            *[pltpu.VMEM((4, 2, 48, n), bf16) for n in cols],
-            *[pltpu.VMEM((4, 2, 48, n), bf16) for n in cols],
-            *[pltpu.VMEM((4, 48, n), f32) for n in cols],
-            *[pltpu.VMEM((4, 24, n), f32) for n in cols],
-            pltpu.VMEM((3, rows, D), f32),
-            pltpu.VMEM((7, rows, D), f32),
-            pltpu.VMEM((rows, D), f32),
-            pltpu.VMEM((rows, D), f32),
-            pltpu.VMEM((rows, D), f32),
-            *sems(11 * (count + 1)),
-        ],
-        compiler_params=params(ident),
-    )(*arrays, small)
-
-
 def heads_in(ref, scratch):
     for h in range(HEADS):
         scratch[pl.ds(h * TOK, TOK), :] = ref[:, pl.ds(h * HD, HD)]
@@ -565,16 +369,91 @@
     )(queries, kv, start, ids)
 
 
-def attend_back_kernel(q_in, kv, g_in, exact, start, ids, lse, dq, dkv, q, g, acc):
+def three(ref):
+    return ref[0].astype(f32) + ref[1].astype(f32) + ref[2].astype(f32)
+
+
+def back_kernel(*refs):
+    (q_in, kv, exact, start, ids, lse, grad_resid, w_out, attn_low, cosine, sine, normed, inverse) = refs[:13]
+    gain, resid, mlp_gain_terms, w_qkv_hbm, act_hbm, *terms, down_terms = refs[13:22]
+    in_grad, layer_out, sum_gate, sum_up, sum_down, sum_qkv, sum_out, small_out = refs[22:30]
+    (q, g, acc, dkv, cb, s, r1a, r1b, ta, tb, r2a, r2b, u, r3, w_qkv, act_all, gb_all, al_heads, al_all) = refs[30:49]
+    gp, gp_flat, gp_all, part, part_other, small, e1, e2, e3, f1, f2 = refs[49:60]
+    own, first_in, mid, second_in, summed, third_in = (refs[60 + 3 * k : 63 + 3 * k] for k in range(6))
+    q_terms, q_first, q_mid, q_second, q_summed, q_third = refs[78:84]
+    down_own, down_core, down_sent, down_in, down_part, down_other, send_sems, recv_sems, local_sems = refs[84:]
+
     me = here()
-    shard = ((me["z"] * 4 + me["y"]) * 2 + me["xh"]) * 2 + me["c"]
-    last = shard // BLOCK_SHARDS
+    z, y, xh, c, n = (me[a] for a in AXES)
+    shard = ((z * 4 + y) * 2 + xh) * 2 + c
+    partner, across, other = at(me, c=1), at(me, xh=1), at(me, n=1)
+    ys = {d: at(me, y=d) for d in (1, 2, 3)}
+    zs = {d: at(me, z=d) for d in (1, 2, 3)}
+    near_moves = [(d, e) for d in (1, 3, 2, 0) for e in (0, 1) if d or e]
+    near = {m: at(me, y=m[0], xh=m[1]) for m in near_moves}
+    group = {m: at(me, y=m[0], c=m[1]) for m in near_moves}
+    greet([other, *zs.values(), *near.values(), *(group[m] for m in near_moves if m[1])])
+    copies = Copies(send_sems, recv_sems)
+    half = TOK // 2
+    low, high = pl.ds(0, half), pl.ds(half, half)
+
+    local = []
+
+    def load(src, dst):
+        copy = pltpu.make_async_copy(src, dst, local_sems.at[len(local)])
+        copy.start()
+        local.append(copy)
+        return copy
+
+    def z_rows(d):
+        return pl.ds(pl.multiple_of(step(me, "z", d) * 384, 384), 384)
+
+    first = {}
+
+    def send_first(i, d):
+        first[i, d] = copies.send(terms[i].at[z_rows(d)], first_in[i].at[d - 1], zs[d])
+
+    for d in (1, 3, 2):
+        send_first(0, d)
+    for d in (1, 3):
+        send_first(1, d)
+
+    branch = grad_resid[...].astype(bf16)
+    gb_all[y, c] = branch
+    mine = pl.ds(pl.multiple_of(half * n, half), half)
+    theirs = pl.ds(pl.multiple_of(half * (1 - n), half), half)
+    gathered = {d: copies.send(gb_all.at[y, c, mine], gb_all.at[y, c, mine], ys[d]) for d in (1, 3, 2)}
+    gb_core = [copies.send(gb_all.at[y, c], gb_all.at[y, c], partner)]
+    for h in range(HEADS):
+        al_heads[h] = attn_low[:, pl.ds(h * HD, HD)]
+
+    def head_of(d, e):
+        taker = step(me, "y", d) * 2 + step(me, "c", e)
+        return jnp.where(taker < HEADS, taker, 0)
+
+    al_moves = [
+        copies.send(al_heads.at[head_of(*m)], al_all.at[y, c], group[m]) for m in near_moves
+    ]
+    al_all[y, c] = al_heads[head_of(0, 0)]
+    load_w = load(w_qkv_hbm, w_qkv)
+    load_act = load(act_hbm, act_all)
+    load_own = [load(terms[i].at[z_rows(0)], own[i]) for i in range(3)]
+    down_cores = {}
+    load_down = {}
+    for d in (2, 1, 3, 0):
+        yi = step(me, "y", d)
+        down_cores[d] = copies.send(down_terms.at[yi, 1 - c], down_core.at[d], partner)
+        load_down[d] = load(down_terms.at[yi, c], down_own.at[d])
+
     heads_in(q_in, q)
-    heads_in(g_in, g)
+    grads_in = nt(branch, w_out[...]).astype(bf16)
+    for h in range(HEADS):
+        g[pl.ds(h * TOK, TOK), :] = grads_in[:, h * HD : (h + 1) * HD]
     balance = jnp.sum(g[...].astype(f32).T * exact[...], axis=0, keepdims=True)
     acc[...] = jnp.zeros_like(acc)
-    total = lse[...]
-    earlier = jnp.where(start[...] < last * KEY_BLOCK, total, -big_negative)
+    last = shard // BLOCK_SHARDS
+    log_total = lse[...]
+    earlier = jnp.where(start[...] < last * KEY_BLOCK, log_total, -big_negative)
 
     def block(index, masked, shift):
         offset = pl.multiple_of(index * KEY_BLOCK, KEY_BLOCK)
@@ -585,19 +464,21 @@
         dv = jnp.zeros((KEY_BLOCK, HD), f32)
         for chunk in range(NQ // Q_CHUNK):
             cs = pl.ds(chunk * Q_CHUNK, Q_CHUNK)
-            part = slice(chunk * Q_CHUNK, (chunk + 1) * Q_CHUNK)
+            piece = slice(chunk * Q_CHUNK, (chunk + 1) * Q_CHUNK)
             qc, gc = q[cs, :], g[cs, :]
-            probs = jnp.exp2(nt(keys, qc) * SCALE_LOG2 - shift[:, part])
+            probs = jnp.exp2(nt(keys, qc) * SCALE_LOG2 - shift[:, piece])
             if masked:
                 key_ids = offset + lax.broadcasted_iota(jnp.int32, (KEY_BLOCK, Q_CHUNK), 0)
                 allowed = (key_ids >= start[:, cs]) & (key_ids <= ids[:, cs])
                 probs = jnp.where(allowed, probs, 0.0)
-            grads = (probs * (nt(values, gc) - balance[:, part])).astype(bf16)
+            grads = (probs * (nt(values, gc) - balance[:, piece])).astype(bf16)
             dv = dv + nn(probs.astype(bf16), gc)
             dk = dk + nn(grads, qc)
             acc[:, cs] = acc[:, cs] + nn(keys_t, grads)
-        dkv[rows, pl.ds(0, HD)] = (dk * SCALE).astype(bf16)
-        dkv[rows, pl.ds(HD, HD)] = dv.astype(bf16)
+        zi, yi = index // 4, lax.rem(index, 4)
+        shape = (2, 2, TOK, HD)
+        dkv[zi, yi, :, :, :, pl.ds(0, HD)] = (dk * SCALE).astype(bf16).reshape(shape)
+        dkv[zi, yi, :, :, :, pl.ds(HD, HD)] = dv.astype(bf16).reshape(shape)
 
     @pl.when(last > 0)
     def _():
@@ -607,35 +488,274 @@
         def _(index):
             block(index, False, earlier)
 
-    block(last, True, total)
+    block(last, True, log_total)
 
     @pl.loop(last + 1, TOKENS // KEY_BLOCK)
     def _(index):
-        dkv[pl.ds(pl.multiple_of(index * KEY_BLOCK, KEY_BLOCK), KEY_BLOCK), :] = jnp.zeros(
-            (KEY_BLOCK, 2 * HD), bf16
-        )
-
-    rows = (acc[...] * SCALE).T
+        dkv[index // 4, lax.rem(index, 4)] = jnp.zeros((2, 2, TOK, 2 * HD), bf16)
+
+    kv_cores = [
+        copies.send(dkv.at[:, :, :, 1 - c, rows], cb.at[:, :, :, rows], partner)
+        for rows in (low, high)
+    ]
+    first_a, first_b, second_a, second_b = {}, {}, {}, {}
+    for rows, core in ((low, kv_cores[0]), (high, kv_cores[1])):
+        core.wait_recv()
+        for zi in range(4):
+            s[zi, :, :, rows] = (dkv[zi, :, :, c, rows].astype(f32) + cb[zi, :, :, rows].astype(f32)).astype(bf16)
+        for d in (1, 3, 2):
+            if rows is low:
+                first_a[d] = copies.send(s.at[step(me, "z", d), :, :, low], r1a.at[d - 1], zs[d])
+            else:
+                first_b[d] = copies.send(s.at[:, step(me, "y", d), :, high], r1b.at[d - 1], ys[d])
+
+    for i, d in ((1, 2), (2, 1), (2, 3), (2, 2)):
+        send_first(i, d)
+    turned_back = (acc[...] * SCALE).T
+
+    def revert(rows):
+        return rows * cosine[...] - pltpu.roll(rows, HD // 2, 1) * sine[...]
+
+    def keep_head(h, rows):
+        low_rows = rows.astype(bf16)
+        gp[h] = low_rows
+        gp_flat[:, pl.ds(h * HD, HD)] = low_rows
+        small[pl.ds(2, 1), pl.ds(h * HD, HD)] = jnp.sum(low_rows.astype(f32), axis=0, keepdims=True)
+
+    small[...] = jnp.zeros_like(small)
+    small[pl.ds(1, 1), :] = mlp_gain_terms[...]
     for h in range(HEADS):
-        dq[:, pl.ds(h * HD, HD)] = rows[h * TOK : (h + 1) * TOK]
-
-
-def attend_back(queries, kv, grads, exact, start, ids, lse):
+        keep_head(h, revert(turned_back[h * TOK : (h + 1) * TOK]))
+    gb_other = {}
+    for d in (1, 3, 2):
+        gathered[d].wait_recv()
+        slot = gb_all.at[lax.rem(y + (4 - d), 4), c, mine]
+        gb_other[d] = copies.send(slot, slot, other)
+        gb_core.append(copies.send(slot, slot, partner))
+    load_w.wait()
+    front = HEADS * HD
+    partial = nt(gp_flat[:, pl.ds(0, front)], w_qkv[:, pl.ds(0, front)])
+
+    for d in (1, 3, 2):
+        first_a[d].wait_recv()
+    ta[...] = (s[z, :, :, low].astype(f32) + three(r1a)).astype(bf16)
+    for d in (1, 3, 2):
+        second_a[d] = copies.send(ta.at[step(me, "y", d)], r2a.at[d - 1], ys[d])
+    for d in (1, 3, 2):
+        first_b[d].wait_recv()
+    tb[...] = (s[:, y, :, high].astype(f32) + three(r1b)).astype(bf16)
+    for d in (1, 3, 2):
+        second_b[d] = copies.send(tb.at[step(me, "z", d)], r2b.at[d - 1], zs[d])
+    for d in (1, 3, 2):
+        second_a[d].wait_recv()
+        second_b[d].wait_recv()
+    ua = ta[y].astype(f32) + three(r2a)
+    ub = tb[z].astype(f32) + three(r2b)
+    u[:, low] = ua.astype(bf16)
+    u[:, high] = ub.astype(bf16)
+    kv_last = copies.send(u.at[1 - xh], r3, across)
+
+    down_moves = {}
+    for d in (2, 1, 3):
+        down_cores[d].wait_recv()
+        load_down[d].wait()
+        down_sent[d - 1] = (down_own[d].astype(f32) + down_core[d].astype(f32)).astype(bf16)
+
+    kv_last.wait_recv()
+    grad_kv = u[xh].astype(f32) + r3[...].astype(f32)
+    keep_head(HEADS, revert(grad_kv[:, :HD]))
+    keep_head(HEADS + 1, grad_kv[:, HD:])
+    gp_moves = [
+        copies.send(gp.at[step(me, "y", m[0]) * 2 + step(me, "c", m[1])], gp_all.at[y, c], group[m])
+        for m in near_moves
+    ]
+    gp_all[y, c] = gp[y * 2 + c]
+    back = pl.ds(front, 2 * HD)
+    part[...] = (partial + nt(gp_flat[:, back], w_qkv[:, back])).astype(bf16)
+    swap = copies.send(part, part_other, other)
+    for d in (2, 1, 3):
+        down_moves[d] = copies.send(down_sent.at[d - 1], down_in.at[d - 1], ys[d])
+
+    for d in (1, 3, 2):
+        gb_other[d].wait_recv()
+        slot = gb_all.at[lax.rem(y + (4 - d), 4), c, theirs]
+        gb_core.append(copies.send(slot, slot, partner))
+    load_act.wait()
+    for copy in gp_moves:
+        copy.wait_recv()
+    q_terms[pl.ds(0, HD), :] = tn(
+        gp_all[...].reshape(GROUP * TOK, HD), act_all[...].reshape(GROUP * TOK, D)
+    ).astype(bf16)
+
+    def z_cols(d):
+        return pl.ds(pl.multiple_of(step(me, "z", d) * 384, 384), 384)
+
+    q_one = {d: copies.send(q_terms.at[pl.ds(0, HD), z_cols(d)], q_first.at[d - 1, pl.ds(0, HD)], zs[d]) for d in (1, 3, 2)}
+    for copy in al_moves + gb_core:
+        copy.wait_recv()
+    q_terms[pl.ds(HD, HD), :] = tn(
+        al_all[...].reshape(GROUP * TOK, HD), gb_all[...].reshape(GROUP * TOK, D)
+    ).astype(bf16)
+    q_two = {d: copies.send(q_terms.at[pl.ds(HD, HD), z_cols(d)], q_first.at[d - 1, pl.ds(HD, HD)], zs[d]) for d in (1, 3, 2)}
+
+    swap.wait_recv()
+    grad_act = part[...].astype(f32) + part_other[...].astype(f32)
+    small[pl.ds(0, 1), :] = jnp.sum(grad_act * normed[...], axis=0, keepdims=True)
+    small_one = {d: copies.send(small, e1.at[d - 1], zs[d]) for d in (1, 3, 2)}
+    grad_normed = grad_act * gain[...]
+    inner = jnp.mean(grad_normed * normed[...], axis=-1, keepdims=True)
+    in_grad[...] = (grad_resid[...] + inverse[...] * (grad_normed - normed[...] * inner)).astype(bf16)
+
+    second = {}
+
+    def send_second(i, mid_ref, in_ref):
+        for m in near_moves:
+            second[i, m] = copies.send(
+                mid_ref.at[step(me, "y", m[0]), step(me, "xh", m[1])], in_ref.at[y, xh], near[m]
+            )
+        in_ref[y, xh] = mid_ref[y, xh]
+
+    for d in (1, 3, 2):
+        small_one[d].wait_recv()
+    f1[...] = small[...] + three(e1)
+    small_two = {m: copies.send(f1, e2.at[k], near[m]) for k, m in enumerate(near_moves)}
+    for i in range(3):
+        load_own[i].wait()
+        for d in (1, 3, 2):
+            first[i, d].wait_recv()
+        for yi in range(4):
+            for xi in range(2):
+                rows = pl.ds(96 * yi + 48 * xi, 48)
+                total = own[i][rows].astype(f32)
+                for d in range(3):
+                    total = total + first_in[i][d, rows].astype(f32)
+                mid[i][yi, xi] = total.astype(bf16)
+        send_second(i, mid[i], second_in[i])
+    for d in (1, 3, 2):
+        q_one[d].wait_recv()
+        q_two[d].wait_recv()
+    q_sum = (q_terms[:, z_cols(0)].astype(f32) + three(q_first)).T.astype(bf16)
+    for yi in range(4):
+        for xi in range(2):
+            q_mid[yi, xi] = q_sum[96 * yi + 48 * xi : 96 * yi + 48 * xi + 48]
+    send_second(3, q_mid, q_second)
+
+    load_down[0].wait()
+    down_cores[0].wait_recv()
+    mlp_out = down_own[0].astype(f32) + down_core[0].astype(f32)
+    for d in (1, 3, 2):
+        down_moves[d].wait_recv()
+        mlp_out = mlp_out + down_in[d - 1].astype(f32)
+    down_part[...] = mlp_out.astype(bf16)
+    down_swap = copies.send(down_part, down_other, other)
+
+    for m in near_moves:
+        small_two[m].wait_recv()
+    f2[...] = f1[...]
+    for k in range(len(near_moves)):
+        f2[...] = f2[...] + e2[k]
+    small_three = copies.send(f2, e3, partner)
+    keep, give = pl.ds(pl.multiple_of(24 * c, 8), 24), pl.ds(pl.multiple_of(24 * (1 - c), 8), 24)
+    third = []
+    all_summed = [*summed, q_summed]
+    all_second = [*second_in, q_second]
+    all_third = [*third_in, q_third]
+    for i in range(4):
+        for m in near_moves:
+            second[i, m].wait_recv()
+        all_summed[i][...] = all_second[i][:, 0].astype(f32) + all_second[i][:, 1].astype(f32)
+        third.append(copies.send(all_summed[i].at[:, give], all_third[i], partner))
+    for i, outs in enumerate(((sum_gate,), (sum_up,), (sum_down,), (sum_qkv, sum_out))):
+        third[i].wait_recv()
+        for yi in range(4):
+            mine_sum, their_sum = all_summed[i][yi, keep], all_third[i][yi]
+            pair = (jnp.where(c == 0, mine_sum, their_sum), jnp.where(c == 0, their_sum, mine_sum))
+            for e in range(2):
+                k = 2 * yi + e
+                if i < 3:
+                    outs[0][:, pl.ds(k * UNITS, UNITS)] = pair[e]
+                else:
+                    outs[0][:, pl.ds(k * HD, HD)] = pair[e][:, :HD]
+                    if k < HEADS:
+                        outs[1][:, pl.ds(k * HD, HD)] = pair[e][:, HD:]
+    small_three.wait_recv()
+    small_out[...] = f2[...] + e3[...]
+    down_swap.wait_recv()
+    layer_out[...] = (
+        resid[...] + (down_part[...].astype(f32) + down_other[...].astype(f32))
+    ).astype(bf16)
+    copies.finish()
+
+
+def back(*arrays):
+    half = TOK // 2
+    wide = 2 * HD
     return pl.pallas_call(
-        attend_back_kernel,
-        out_shape=(
-            jax.ShapeDtypeStruct((TOK, HEADS * HD), f32),
-            jax.ShapeDtypeStruct((TOKENS, 2 * HD), bf16),
-        ),
-        in_specs=[VMEM] * 7,
-        out_specs=(VMEM,) * 2,
+        back_kernel,
+        out_shape=[
+            jax.ShapeDtypeStruct((TOK, D), bf16),
+            jax.ShapeDtypeStruct((TOK, D), bf16),
+            *[jax.ShapeDtypeStruct((24, FF // 2), f32)] * 3,
+            jax.ShapeDtypeStruct((24, (HEADS + 2) * HD), f32),
+            jax.ShapeDtypeStruct((24, HEADS * HD), f32),
+            jax.ShapeDtypeStruct((8, D), f32),
+        ],
+        in_specs=[VMEM] * 16 + [ANY] * 6,
+        out_specs=[VMEM] * 8,
         scratch_shapes=[
             pltpu.VMEM((NQ, HD), bf16),
             pltpu.VMEM((NQ, HD), bf16),
             pltpu.VMEM((HD, NQ), f32),
+            pltpu.VMEM((4, 4, 2, 2, TOK, wide), bf16),
+            pltpu.VMEM((4, 4, 2, TOK, wide), bf16),
+            pltpu.VMEM((4, 4, 2, TOK, wide), bf16),
+            pltpu.VMEM((3, 4, 2, half, wide), bf16),
+            pltpu.VMEM((3, 4, 2, half, wide), bf16),
+            pltpu.VMEM((4, 2, half, wide), bf16),
+            pltpu.VMEM((4, 2, half, wide), bf16),
+            pltpu.VMEM((3, 2, half, wide), bf16),
+            pltpu.VMEM((3, 2, half, wide), bf16),
+            pltpu.VMEM((2, TOK, wide), bf16),
+            pltpu.VMEM((TOK, wide), bf16),
+            pltpu.VMEM((D, (HEADS + 2) * HD), bf16),
+            pltpu.VMEM((4, 2, TOK, D), bf16),
+            pltpu.VMEM((4, 2, TOK, D), bf16),
+            pltpu.VMEM((HEADS, TOK, HD), bf16),
+            pltpu.VMEM((4, 2, TOK, HD), bf16),
+            pltpu.VMEM((HEADS + 2, TOK, HD), bf16),
+            pltpu.VMEM((TOK, (HEADS + 2) * HD), bf16),
+            pltpu.VMEM((4, 2, TOK, HD), bf16),
+            pltpu.VMEM((TOK, D), bf16),
+            pltpu.VMEM((TOK, D), bf16),
+            pltpu.VMEM((8, D), f32),
+            pltpu.VMEM((3, 8, D), f32),
+            pltpu.VMEM((7, 8, D), f32),
+            pltpu.VMEM((8, D), f32),
+            pltpu.VMEM((8, D), f32),
+            pltpu.VMEM((8, D), f32),
+            *[pltpu.VMEM((384, UNITS), bf16)] * 3,
+            *[pltpu.VMEM((3, 384, UNITS), bf16)] * 3,
+            *[pltpu.VMEM((4, 2, 48, UNITS), bf16)] * 3,
+            *[pltpu.VMEM((4, 2, 48, UNITS), bf16)] * 3,
+            *[pltpu.VMEM((4, 48, UNITS), f32)] * 3,
+            *[pltpu.VMEM((4, 24, UNITS), f32)] * 3,
+            pltpu.VMEM((wide, D), bf16),
+            pltpu.VMEM((3, wide, 384), bf16),
+            pltpu.VMEM((4, 2, 48, wide), bf16),
+            pltpu.VMEM((4, 2, 48, wide), bf16),
+            pltpu.VMEM((4, 48, wide), f32),
+            pltpu.VMEM((4, 24, wide), f32),
+            pltpu.VMEM((4, TOK, D), bf16),
+            pltpu.VMEM((4, TOK, D), bf16),
+            pltpu.VMEM((3, TOK, D), bf16),
+            pltpu.VMEM((3, TOK, D), bf16),
+            pltpu.VMEM((TOK, D), bf16),
+            pltpu.VMEM((TOK, D), bf16),
+            *sems(140),
+            pltpu.SemaphoreType.DMA((9,)),
         ],
-        compiler_params=pltpu.CompilerParams(vmem_limit_bytes=60 * 2**20),
-    )(queries, kv, grads, exact, start, ids, lse)
+        compiler_params=params(9, 62),
+    )(*arrays)
 
 
 def row_starts(lengths, token_ids):
@@ -700,9 +820,8 @@
     resid = input_f32 + narrow_sum(3, nn(attn_low, w_out).astype(bf16))
     normed_mlp, inverse_mlp = normalize(resid)
     act_mlp = (normed_mlp * norm_mlp).astype(bf16)
-    act_all, out_grad_all = (
-        a.reshape(GROUP * TOK, D) for a in group_gather(4, [act_mlp, out_grad])
-    )
+    act_all, out_grad_all, act_attn_all = group_gather(4, [act_mlp, out_grad, act_attn])
+    act_all, out_grad_all = act_all.reshape(GROUP * TOK, D), out_grad_all.reshape(GROUP * TOK, D)
     gate = nn(act_all, gate_w)
     up = nn(act_all, up_w)
     sigmoid = jax.nn.sigmoid(gate)
@@ -713,55 +832,19 @@
     grad_up_pre = (grad_hidden * silu).astype(bf16)
     down_terms = nn(hidden, down_w).astype(bf16).reshape(4, 2, TOK, D)
     back_terms = (nt(grad_gate_pre, gate_w) + nt(grad_up_pre, up_w)).astype(bf16)
-    mlp_out, grad_act_mlp = group_reduce(5, [down_terms, back_terms.reshape(4, 2, TOK, D)])
-    layer_out = (resid + mlp_out).astype(bf16)
+    (grad_act_mlp,) = group_reduce(5, [back_terms.reshape(4, 2, TOK, D)])
     grad_norm_mlp = jnp.sum(grad_act_mlp * normed_mlp, axis=0)
     grad_resid = out_grad.astype(f32) + norm_back(
         grad_act_mlp * norm_mlp, normed_mlp, inverse_mlp
     )
-    grad_branch = grad_resid.astype(bf16)
-    grad_attn = nt(grad_branch, w_out).astype(bf16)
-    grad_q, grad_kv_terms = attend_back(queries, kv, grad_attn, exact, start, ids, lse)
-    grad_kv = kv_reduce(grad_kv_terms.reshape(4, 4, 2, 2, TOK, 2 * HD))
-    grad_turned = jnp.concatenate([grad_q, grad_kv[:, :HD]], axis=1)
-    grad_projected = jnp.concatenate(
-        [rotate(grad_turned, cosine, -sine), grad_kv[:, HD:]], axis=1
-    ).astype(bf16)
-    grad_act_attn = narrow_sum(6, nt(grad_projected, w_qkv).astype(bf16))
-    grad_norm_attn = jnp.sum(grad_act_attn * normed_attn, axis=0)
-    in_grad = (
-        grad_resid + norm_back(grad_act_attn * norm_attn, normed_attn, inverse_attn)
-    ).astype(bf16)
-
-    act_attn_all, branch_all = (
-        a.reshape(GROUP * TOK, D) for a in group_gather(7, [act_attn, grad_branch])
-    )
-    by_head = grad_projected.reshape(TOK, 4, 2, HD).transpose(1, 2, 0, 3)
-    low_cols = attn_low.reshape(TOK, 4, 2, OUT_COLS).transpose(1, 2, 0, 3)
-    head_grads, low_all = (
-        a.reshape(GROUP * TOK, -1) for a in group_swap(8, [by_head, low_cols])
-    )
-    bias_sums = jnp.sum(grad_projected.astype(f32), axis=0)
-    small = jnp.concatenate(
-        [
-            grad_norm_attn[None],
-            grad_norm_mlp[None],
-            jnp.pad(bias_sums, (0, D - bias_sums.shape[0]))[None],
-            jnp.zeros((5, D), f32),
-        ]
-    )
     terms = [
-        tn(act_all, grad_gate_pre),
-        tn(act_all, grad_up_pre),
-        tn(out_grad_all, hidden),
-        tn(act_attn_all, head_grads),
-        tn(branch_all, low_all),
+        t.astype(bf16)
+        for t in (tn(act_all, grad_gate_pre), tn(act_all, grad_up_pre), tn(out_grad_all, hidden))
     ]
-    *sums, small = weight_reduce(
-        9, [t.astype(bf16).reshape(4, D // 4, t.shape[1]) for t in terms], small
-    )
-    sum_gate, sum_up, sum_down, sum_qkv, sum_out = (
-        s.transpose(2, 0, 1, 3).reshape(24, -1) for s in sums
+    in_grad, layer_out, sum_gate, sum_up, sum_down, sum_qkv, sum_out, small = back(
+        queries, kv, exact, start, ids, lse, grad_resid, w_out, attn_low, cosine, sine, normed_attn,
+        inverse_attn[:, None], norm_attn[None], resid, grad_norm_mlp[None],
+        w_qkv, act_attn_all, *terms, down_terms,
     )
     norms = lax.dynamic_slice(small, (0, shard * 24), (2, 24))
     bias = lax.dynamic_slice(

time: 514 us -> 400 us (0.78)
  Pallas kernels: 372 us -> 307 us
  local copies, waits for them, and re-layouts: 51.9 us -> 24 us
  matrix products: 61.4 us -> 48.3 us
  other arithmetic: 21.9 us -> 13.5 us
    pallas_call x2 -> x1, Pallas kernels: 83.5 us -> 59.9 us  [group_gather(): pl.pallas_call(functools.partial(group_gather_kernel, count), out_shape=[...]
    pallas_call x1, Pallas kernels: 53.9 us -> 35.6 us  [group_reduce(): pl.pallas_call(functools.partial(group_reduce_kernel, count), out_shape=[...]
    reshape x6 -> x0, local copies, waits for them, and re-layouts: 12 us -> none  [the longest x5 10.2 us: shards(): s.transpose(2, 0, 1, 3).reshape(24, -1)]
    pallas_call x4 -> x1, Pallas kernels: 173 us -> 161 us  [back(): pl.pallas_call(back_kernel, out_shape=[jax.ShapeDtypeStruct((TOK, D), bf1...]
    pallas_call x2 -> x1, Pallas kernels: 23.6 us -> 12.7 us  [narrow_sum(): pl.pallas_call(narrow_sum_kernel, out_shape=jax.ShapeDtypeStruct(array.sh...]
    dot_general x5 -> x3, matrix products: 21 us -> 10.3 us  [tn(): lax.dot_general(a, b, (((0,), (0,)), ((), ())), preferred_element_type=f32)]
    convert_element_type x6 -> x3, local copies, waits for them, and re-layouts: 17.4 us -> 7.08 us  [shards(): t.astype(bf16)]
    unnamed x52 -> x41, local copies, waits for them, and re-layouts: 0.99 us -> 11 us
where the time goes in v2:
time: 400 us; the launch traced here: 395 us
  Pallas kernels  307 us (77%)
  matrix products  48.3 us (12%)
  local copies, waits for them, and re-layouts  24 us (6%)
  other arithmetic  13.5 us (3%)
    pallas_call x1, Pallas kernels, back(): pl.pallas_call(back_kernel, out_shape=[jax.ShapeDtypeStruct((TOK, D), bf1...  161 us
    pallas_call x1, Pallas kernels, group_gather(): pl.pallas_call(functools.partial(group_gather_kernel, count), out_shape=[...  59.9 us
    pallas_call x1, Pallas kernels, group_reduce(): pl.pallas_call(functools.partial(group_reduce_kernel, count), out_shape=[...  35.6 us
    pallas_call x1, Pallas kernels, kv_gather(): pl.pallas_call(kv_gather_kernel, out_shape=jax.ShapeDtypeStruct((4, 4, 2,...  33.1 us
    dot_general x5, matrix products, nn(): lax.dot_general(a, b, (((1,), (0,)), ((), ())), preferred_element_type=f32)  21.4 us
    dot_general x3, matrix products, nt(): lax.dot_general(a, b, (((1,), (1,)), ((), ())), preferred_element_type=f32)  16.6 us
    pallas_call x1, Pallas kernels, narrow_sum(): pl.pallas_call(narrow_sum_kernel, out_shape=jax.ShapeDtypeStruct(array.sh...  12.7 us
    unnamed x41, local copies, waits for them, and re-layouts  11 us

profile of v2, /device:TPU:1, one launch (start us, length us, event | category | flops | bytes accessed | tf_op | source)
XLA Modules:
  0.0 394.5 jit_solution(10797520790711435901)
XLA Ops:
  3.4 2.0 convert_multiply_fusion
  5.4 2.7 convolution_add_fusion
  10.7 33.1 %shard_map.194 = bf16[4,4,2,2,128,256]{5,4,3,2,1,0:T(8,128)(2,1)} custom-call(bf16[128,256]{1,0:T(8,128)(2,1)} %pad_maximum_fusion.2.x), custom_call_target="tpu_custom_call" | custom-call | tf_op jit(solution)/shard_map/pallas_call | solution.py:163
  44.5 4.7 %shard_map.195 = (bf16[128,768]{1,0:T(8,128)(2,1)}, f32[128,768]{1,0:T(8,128)}, f32[1,768]{1,0:T(1,128)}) custom-call(bf16[128,768]{1,0:T(8,128)(2,1)} %copy-done.6, bf16[8192,256]{1,0:T(8,128)(2,1)} %bitcast.45, s32[1,768]{1,0:T(1,128)} %get-tuple-element.89.start.refs_3_, s32[1,768]{1,0:T(1,128)} %get-tuple-element.88.ids.refs_4_), custom_call_target="tpu_custom_call" | custom-call | tf_op jit(solution)/shard_map/pallas_call | solution.py:352
  49.2 2.2 convolution_convert_fusion.4.x
  51.4 12.7 %shard_map.196 = f32[128,1536]{1,0:T(8,128)} custom-call(bf16[128,1536]{1,0:T(8,128)(2,1)} %convolution_convert_fusion.4.x), custom_call_target="tpu_custom_call" | custom-call | tf_op jit(solution)/shard_map/pallas_call | solution.py:276
  66.4 59.9 %shard_map.197 = (bf16[4,2,128,1536]{3,2,1,0:T(8,128)(2,1)}, bf16[4,2,128,1536]{3,2,1,0:T(8,128)(2,1)}, bf16[4,2,128,1536]{3,2,1,0:T(8,128)(2,1)}) custom-call(bf16[128,1536]{1,0:T(8,128)(2,1)} %multiply_convert_fusion.3.refs_0_, bf16[128,1536]{1,0:T(8,128)(2,1)} %refs_1_.1, bf16[128,1536]{1,0:T(8,128)(2,1)} %copy-done.3), custom_call_target="tpu_custom_call" | custom-call | tf_op jit(solution)/shard_map/pallas_call | solution.py:202
  126.4 4.5 %fusion.9 = f32[1024,560]{0,1:T(8,128)S(1)} fusion(bf16[1024,1536]{1,0:T(8,128)(2,1)} %bitcast.61, bf16[4480,1536]{1,0:T(8,128)(2,1)} %param.20, s32[]{:T(128)S(6)} %select_n.16), kind=kOutput, calls=%fused_computation.19 | convolution fusion | flops 1761607680 | bytes 7159812 | tf_op jit(solution)/shard_map/dot_general | solution.py:50
  130.9 4.3 %fusion.3 = f32[1024,560]{0,1:T(8,128)S(1)} fusion(bf16[1024,1536]{1,0:T(8,128)(2,1)S(1)} %bitcast.59, bf16[1536,4480]{1,0:T(8,128)(2,1)} %param.18, s32[]{:T(128)S(6)} %select_n.16), kind=kOutput, calls=%fused_computation.13 | convolution fusion | flops 1761607680 | bytes 7405572 | tf_op jit(solution)/shard_map/dot_general | solution.py:46
  135.2 6.8 %multiply_convert_fusion = (bf16[1024,560]{0,1:T(8,128)(2,1)S(1)}, bf16[1024,560]{0,1:T(8,128)(2,1)}, bf16[1024,560]{0,1:T(8,128)(2,1)}) fusion(f32[1024,560]{0,1:T(8,128)S(1)} %fusion.3, f32[1024,560]{0,1:T(8,128)S(1)} %fusion.9, bf16[1024,1536]{1,0:T(8,128)(2,1)S(1)} %bitcast.60, bf16[1536,4480]{1,0:T(8,128)(2,1)} %param.19, s32[]{:T(128)S(6)} %select_n.16), kind=kOutput, calls=%fused_computation.6 | convolution fusion | flops 1770209280 | bytes 13139972 | tf_op jit(solution)/shard_map/dot_general | solution.py:46
  143.0 1.9 convolution_convert_fusion.1
  145.0 2.5 copy.35.refs_20_
  147.5 4.2 %convolution_convert_fusion.2 = bf16[1536,560]{0,1:T(8,128)(2,1)S(1)} fusion(bf16[1024,560]{0,1:T(8,128)(2,1)} %get-tuple-element.47, bf16[1024,1536]{1,0:T(8,128)(2,1)} %bitcast.57), kind=kOutput, calls=%fused_computation.3 | convolution fusion | flops 1762467840 | bytes 6012928 | tf_op jit(solution)/shard_map/dot_general | solution.py:54
  151.7 2.3 copy.34.refs_19_
  153.9 4.2 %convolution_convert_fusion.3 = bf16[1536,560]{0,1:T(8,128)(2,1)S(1)} fusion(bf16[1024,560]{0,1:T(8,128)(2,1)} %get-tuple-element.46, bf16[1024,1536]{1,0:T(8,128)(2,1)} %bitcast.58), kind=kOutput, calls=%fused_computation.4 | convolution fusion | flops 1762467840 | bytes 6012928 | tf_op jit(solution)/shard_map/dot_general | solution.py:54
  158.1 2.3 copy.33.refs_18_
  160.4 5.2 %fusion.1 = f32[1024,1536]{1,0:T(8,128)S(1)} fusion(bf16[1024,560]{0,1:T(8,128)(2,1)} %get-tuple-element.46, bf16[1536,4480]{1,0:T(8,128)(2,1)} %param.18, s32[]{:T(128)S(6)} %select_n.16), kind=kOutput, calls=%fused_computation.11 | convolution fusion | flops 1761607680 | bytes 9404420 | tf_op jit(solution)/shard_map/dot_general | solution.py:50
  165.7 6.9 %add_convert_fusion = bf16[1024,1536]{1,0:T(8,128)(2,1)} fusion(f32[1024,1536]{1,0:T(8,128)S(1)} %fusion.1, bf16[1024,560]{0,1:T(8,128)(2,1)S(1)} %copy-done.13, bf16[1536,4480]{1,0:T(8,128)(2,1)} %param.19, s32[]{:T(128)S(6)} %select_n.16), kind=kOutput, calls=%fused_computation | convolution fusion | flops 1764753408 | bytes 12550148 | tf_op jit(solution)/shard_map/dot_general | solution.py:50
  172.5 35.6 %shard_map.198 = f32[128,1536]{1,0:T(8,128)} custom-call(bf16[4,2,128,1536]{3,2,1,0:T(8,128)(2,1)} %bitcast.48), custom_call_target="tpu_custom_call" | custom-call | tf_op jit(solution)/shard_map/pallas_call | solution.py:248
  209.8 2.3 multiply_add_fusion.refs_6_
  212.7 5.5 %convolution_convert_fusion = bf16[1024,1536]{1,0:T(8,128)(2,1)} fusion(bf16[1024,560]{0,1:T(8,128)(2,1)S(1)} %copy-done.15, bf16[4480,1536]{1,0:T(8,128)(2,1)} %param.20, s32[]{:T(128)S(6)} %select_n.16), kind=kOutput, calls=%fused_computation.1 | convolution fusion | flops 1763180544 | bytes 6012932 | tf_op jit(solution)/shard_map/dot_general | solution.py:46
  219.5 161.3 %shard_map.199 = (bf16[128,1536]{1,0:T(8,128)(2,1)}, bf16[128,1536]{1,0:T(8,128)(2,1)}, f32[24,4480]{1,0:T(8,128)}, f32[24,4480]{1,0:T(8,128)}, f32[24,4480]{1,0...) custom-call(bf16[128,768]{1,0:T(8,128)(2,1)} %copy-done.6, bf16[8192,256]{1,0:T(8,128)(2,1)} %bitcast.46, ...), custom_call_target="tpu_custom_call" | custom-call | tf_op jit(solution)/shard_map/pallas_call | solution.py:693
  384.2 1.8 copy.53
  390.8 1.8 copy.57
  (70 shorter events, 22.5 us)
Async XLA Ops:
  5.4 3.0 copy-start.3
  9.2 34.6 %copy-start.2 = (f32[128,128]{1,0:T(8,128)}, f32[128,128]{1,0:T(8,128)S(1)}, u32[]{:S(2)}) copy-start(f32[128,128]{1,0:T(8,128)S(1)} %get-tuple-element.44.refs_10_) | copy-start | bytes 196612
  10.0 34.5 %copy-start.6 = (bf16[128,768]{1,0:T(8,128)(2,1)}, bf16[128,768]{1,0:T(8,128)(2,1)S(1)}, u32[]{:S(2)}) copy-start(bf16[128,768]{1,0:T(8,128)(2,1)S(1)} %get-tuple-element.49.q_in.refs_0_) | copy-start | bytes 589828
  43.8 5.3 %copy-start.1 = (bf16[768,1536]{1,0:T(8,128)(2,1)S(1)}, bf16[768,1536]{1,0:T(8,128)(2,1)}, u32[]{:S(2)}) copy-start(bf16[768,1536]{1,0:T(8,128)(2,1)} %refs_7_.1) | copy-start | bytes 7077892
  49.2 14.9 %copy-start.4 = (bf16[128,1536]{1,0:T(8,128)(2,1)S(1)}, bf16[128,1536]{1,0:T(8,128)(2,1)}, u32[]{:S(2)}) copy-start(bf16[128,1536]{1,0:T(8,128)(2,1)} %param.11) | copy-start | bytes 1179652
  51.4 14.1 %copy-start.9 = (f32[1536]{0:T(1024)S(1)}, f32[1536]{0:T(1024)}, u32[]{:S(2)}) copy-start(f32[1536]{0:T(1024)} %param.17) | copy-start | bytes 18436
  65.4 144.3 %copy-start = (f32[128,1536]{1,0:T(8,128)}, f32[128,1536]{1,0:T(8,128)S(1)}, u32[]{:S(2)}) copy-start(f32[128,1536]{1,0:T(8,128)S(1)} %get-tuple-element.42.refs_14_) | copy-start | bytes 2359300
  126.4 4.5 %copy-start.11 = (bf16[4,2,128,1536]{3,2,1,0:T(8,128)(2,1)S(1)}, bf16[4,2,128,1536]{3,2,1,0:T(8,128)(2,1)}, u32[]{:S(2)}) copy-start(bf16[4,2,128,1536]{3,2,1,0:T(8,128)(2,1)} %get-tuple-element.29) | copy-start | bytes 9437188
  135.2 7.8 %copy-start.12 = (bf16[4,2,128,1536]{3,2,1,0:T(8,128)(2,1)S(1)}, bf16[4,2,128,1536]{3,2,1,0:T(8,128)(2,1)}, u32[]{:S(2)}) copy-start(bf16[4,2,128,1536]{3,2,1,0:T(8,128)(2,1)} %get-tuple-element.28) | copy-start | bytes 9437188
  142.0 1.0 copy-start.14
  160.4 5.2 %copy-start.13 = (bf16[1024,560]{0,1:T(8,128)(2,1)S(1)}, bf16[1024,560]{0,1:T(8,128)(2,1)}, u32[]{:S(2)}) copy-start(bf16[1024,560]{0,1:T(8,128)(2,1)} %get-tuple-element.47) | copy-start | bytes 3440644
  172.5 37.2 %copy-start.5 = (bf16[128,1536]{1,0:T(8,128)(2,1)S(1)}, bf16[128,1536]{1,0:T(8,128)(2,1)}, u32[]{:S(2)}) copy-start(bf16[128,1536]{1,0:T(8,128)(2,1)} %refs_1_.1) | copy-start | bytes 1179652
  208.2 4.5 %copy-start.15 = (bf16[1024,560]{0,1:T(8,128)(2,1)S(1)}, bf16[1024,560]{0,1:T(8,128)(2,1)}, u32[]{:S(2)}) copy-start(bf16[1024,560]{0,1:T(8,128)(2,1)} %copy-done.14) | copy-start | bytes 3440644
  212.7 6.2 %copy-start.10 = (f32[1536]{0:T(1024)S(1)}, f32[1536]{0:T(1024)}, u32[]{:S(2)}) copy-start(f32[1536]{0:T(1024)} %param.13) | copy-start | bytes 18436
  380.8 11.8 %copy-start.8 = (f32[24,4480]{1,0:T(8,128)S(1)}, f32[24,4480]{1,0:T(8,128)}, u32[]{:S(2)}) copy-start(f32[24,4480]{1,0:T(8,128)} %get-tuple-element.110) | copy-start | bytes 1290244
  380.8 12.5 %copy-start.7 = (f32[24,4480]{1,0:T(8,128)S(1)}, f32[24,4480]{1,0:T(8,128)}, u32[]{:S(2)}) copy-start(f32[24,4480]{1,0:T(8,128)} %get-tuple-element.38) | copy-start | bytes 1290244

commit v3 on v2

v3 whole, which is shorter than its diff:
```python
import functools
import math

import jax
import jax.numpy as jnp
from jax import lax
from jax.experimental import pallas as pl
from jax.experimental.pallas import tpu as pltpu
from jax.sharding import Mesh
from jax.sharding import PartitionSpec as P

HD = 128
QH = 12
KVH = 2
HEADS = QH // KVH
D = 1536
FF = 8960
TOK = 128
TOKENS = 8192
NQ = HEADS * TOK
GROUP = 8
UNITS = FF // 2 // GROUP

AXES = ("z", "y", "xh", "c", "n")
SIZE = {"z": 4, "y": 4, "xh": 2, "c": 2, "n": 2}
WIDE = ("z", "y", "xh", "c")
MESH = pl.DeviceIdType.MESH

rms_eps = 1e-06
rope_base = 10000.0
big_negative = -1e30
SCALE = HD ** (-0.5)
SCALE_LOG2 = SCALE * math.log2(math.e)
KEY_BLOCK = 512
BLOCK_SHARDS = KEY_BLOCK // TOK
Q_CHUNK = 256

bf16 = jnp.bfloat16
f32 = jnp.float32
VMEM = pl.BlockSpec(memory_space=pltpu.VMEM)
SMEM = pl.BlockSpec(memory_space=pltpu.SMEM)
ANY = pl.BlockSpec(memory_space=pl.ANY)


def nn(a, b):
    return lax.dot_general(a, b, (((1,), (0,)), ((), ())), preferred_element_type=f32)


def nt(a, b):
    return lax.dot_general(a, b, (((1,), (1,)), ((), ())), preferred_element_type=f32)


def tn(a, b):
    return lax.dot_general(a, b, (((0,), (0,)), ((), ())), preferred_element_type=f32)


def here():
    return {a: lax.axis_index(a) for a in AXES}


def step(me, axis, by):
    return lax.rem(me[axis] + by, SIZE[axis])


def at(me, **moved):
    return tuple(step(me, a, moved[a]) if a in moved else me[a] for a in AXES)


def greet(peers):
    barrier = pltpu.get_barrier_semaphore()
    for p in peers:
        pl.semaphore_signal(barrier, inc=1, device_id=p, device_id_type=MESH)
    pl.semaphore_wait(barrier, len(peers))


class Copies:
    def __init__(self, send_sems, recv_sems):
        self.send_sems, self.recv_sems, self.used, self.started = send_sems, recv_sems, 0, []

    def make(self, src, dst, target):
        k = self.used
        self.used += 1
        return pltpu.make_async_remote_copy(
            src_ref=src,
            dst_ref=dst,
            send_sem=self.send_sems.at[k],
            recv_sem=self.recv_sems.at[k],
            device_id=target,
            device_id_type=MESH,
        )

    def send(self, src, dst, target):
        copy = self.make(src, dst, target)
        copy.start()
        self.started.append(copy)
        return copy

    def finish(self):
        for copy in self.started:
            copy.wait_send()


def sems(count):
    return [pltpu.SemaphoreType.DMA((count,)), pltpu.SemaphoreType.DMA((count,))]


def params(ident, mib=60):
    return pltpu.CompilerParams(
        collective_id=ident, has_side_effects=True, vmem_limit_bytes=mib * 2**20
    )


def three(ref):
    return ref[0].astype(f32) + ref[1].astype(f32) + ref[2].astype(f32)


def heads_in(ref, scratch):
    for h in range(HEADS):
        scratch[pl.ds(h * TOK, TOK), :] = ref[:, pl.ds(h * HD, HD)]


def shard_of(me):
    return ((me["z"] * 4 + me["y"]) * 2 + me["xh"]) * 2 + me["c"]


class Rows:
    def __init__(self, me, copies, source, slots):
        self.me, self.copies, self.slots = me, copies, slots
        half = TOK // 2
        n = me["n"]
        self.mine = pl.ds(pl.multiple_of(half * n, half), half)
        self.theirs = pl.ds(pl.multiple_of(half * (1 - n), half), half)
        y, c = me["y"], me["c"]
        own = slots.at[y, c]
        self.far = {
            d: copies.send(source.at[self.mine], own.at[self.mine], at(me, y=d)) for d in (1, 3, 2)
        }
        self.near = [copies.send(source, own, at(me, c=1))]
        self.across = {}

    def slot(self, d, rows):
        return self.slots.at[lax.rem(self.me["y"] + (4 - d), 4), self.me["c"], rows]

    def pass_on(self):
        for d in (1, 3, 2):
            self.far[d].wait_recv()
            got = self.slot(d, self.mine)
            self.across[d] = self.copies.send(got, got, at(self.me, n=1))
            self.near.append(self.copies.send(got, got, at(self.me, c=1)))

    def complete(self):
        for d in (1, 3, 2):
            self.across[d].wait_recv()
            got = self.slot(d, self.theirs)
            self.near.append(self.copies.send(got, got, at(self.me, c=1)))

    def wait(self):
        for copy in self.near:
            copy.wait_recv()


def attend_kernel(
    x, q_in, start, ids, og, aa, kv, o, exact, lse, og_all, aa_all,
    q, top, total, acc, low_acc, send_sems, recv_sems, local_sems,
):
    me = here()
    z, y, xh, c = me["z"], me["y"], me["xh"], me["c"]
    partner, across, other = at(me, c=1), at(me, xh=1), at(me, n=1)
    ys = {d: at(me, y=d) for d in (1, 2, 3)}
    zs = {d: at(me, z=d) for d in (1, 2, 3)}
    kv[z, y, xh, c] = x[...]
    greet([partner, across, other, *ys.values(), *zs.values()])
    copies = Copies(send_sems, recv_sems)
    mine = kv.at[z, y, xh, c]
    first = copies.send(mine, mine, across)
    to_core = [copies.send(mine, mine, partner)]
    heads_in(q_in, q)
    top[...] = jnp.full_like(top, big_negative)
    total[...] = jnp.zeros_like(total)
    acc[...] = jnp.zeros_like(acc)
    low_acc[...] = jnp.zeros_like(low_acc)
    first.wait_recv()
    theirs = kv.at[z, y, 1 - xh, c]
    to_core.append(copies.send(theirs, theirs, partner))
    half = TOK // 2
    low, high = pl.ds(0, half), pl.ds(half, half)

    def slot(zi, yi, rows):
        return kv.at[zi, yi, :, c, rows]

    first_low, first_high = {}, {}
    for d in (1, 3, 2):
        first_low[d] = copies.send(slot(z, y, low), slot(z, y, low), ys[d])
        first_high[d] = copies.send(slot(z, y, high), slot(z, y, high), zs[d])
    second_low, second_high = {}, {}
    for e in (0, 1, 3, 2):
        yi, zi = lax.rem(y + (4 - e), 4), lax.rem(z + (4 - e), 4)
        if e:
            first_low[e].wait_recv()
            to_core.append(copies.send(slot(z, yi, low), slot(z, yi, low), partner))
            first_high[e].wait_recv()
            to_core.append(copies.send(slot(zi, y, high), slot(zi, y, high), partner))
        for d in (1, 3, 2):
            second_low[e, d] = copies.send(slot(z, yi, low), slot(z, yi, low), zs[d])
            second_high[e, d] = copies.send(slot(zi, y, high), slot(zi, y, high), ys[d])
    local = []
    for i, (source, slots) in enumerate(((og, og_all), (aa, aa_all))):
        local.append(pltpu.make_async_copy(source, slots.at[y, c], local_sems.at[i]))
        local[-1].start()
    for e in (0, 1, 3, 2):
        for d in (1, 3, 2):
            yi, zi = lax.rem(y + (4 - e), 4), lax.rem(z + (4 - e), 4)
            yd, zd = lax.rem(y + (4 - d), 4), lax.rem(z + (4 - d), 4)
            second_low[e, d].wait_recv()
            to_core.append(copies.send(slot(zd, yi, low), slot(zd, yi, low), partner))
            second_high[e, d].wait_recv()
            to_core.append(copies.send(slot(zi, yd, high), slot(zi, yd, high), partner))
    for copy in to_core:
        copy.wait_recv()
    gathers = [Rows(me, copies, og, og_all), Rows(me, copies, aa, aa_all)]

    last = shard_of(me) // BLOCK_SHARDS

    def block(index, masked):
        zi, yi = index // 4, lax.rem(index, 4)
        shape = (KEY_BLOCK, HD)
        keys = kv[zi, yi, :, :, :, pl.ds(0, HD)].reshape(shape)
        values = kv[zi, yi, :, :, :, pl.ds(HD, HD)].reshape(shape).T
        for chunk in range(NQ // Q_CHUNK):
            cs = pl.ds(chunk * Q_CHUNK, Q_CHUNK)
            scores = nt(keys, q[cs, :]) * SCALE_LOG2
            if masked:
                key_ids = index * KEY_BLOCK + lax.broadcasted_iota(jnp.int32, (KEY_BLOCK, Q_CHUNK), 0)
                allowed = (key_ids >= start[:, cs]) & (key_ids <= ids[:, cs])
                scores = jnp.where(allowed, scores, big_negative)
            old = top[:, cs]
            new = jnp.maximum(old, jnp.max(scores, axis=0, keepdims=True))
            probs = jnp.exp2(scores - new)
            if masked:
                probs = jnp.where(allowed, probs, 0.0)
            fade = jnp.exp2(old - new)
            top[:, cs] = new
            total[:, cs] = total[:, cs] * fade + jnp.sum(probs, axis=0, keepdims=True)
            upper = probs.astype(bf16)
            rest = (probs - upper.astype(f32)).astype(bf16)
            acc[:, cs] = acc[:, cs] * fade + nn(values, upper)
            low_acc[:, cs] = low_acc[:, cs] * fade + nn(values, rest)

    middle = (last + 1) // 2

    @pl.when(last > 0)
    def _():
        block(0, True)

    @pl.loop(1, middle)
    def _(index):
        block(index, False)

    for rows in gathers:
        rows.pass_on()

    @pl.loop(jnp.maximum(middle, 1), last)
    def _(index):
        block(index, False)

    kept = start[...] < last * KEY_BLOCK
    top[...] = jnp.where(kept, top[...], big_negative)
    kept = kept.astype(f32)
    total[...] = total[...] * kept
    acc[...] = acc[...] * kept
    low_acc[...] = low_acc[...] * kept
    block(last, True)
    inverse = 1.0 / total[...]
    rows = acc[...] * inverse
    exact[...] = rows + low_acc[...] * inverse
    rows = rows.T.astype(bf16)
    for h in range(HEADS):
        o[:, pl.ds(h * HD, HD)] = rows[h * TOK : (h + 1) * TOK]
    lse[...] = top[...] + jnp.log2(total[...])
    for rows in gathers:
        rows.complete()
    for rows in gathers:
        rows.wait()
    for copy in local:
        copy.wait()
    copies.finish()


def attend(*arrays):
    slots = jax.ShapeDtypeStruct((4, 2, TOK, D), bf16)
    return pl.pallas_call(
        attend_kernel,
        out_shape=(
            jax.ShapeDtypeStruct((4, 4, 2, 2, TOK, 2 * HD), bf16),
            jax.ShapeDtypeStruct((TOK, HEADS * HD), bf16),
            jax.ShapeDtypeStruct((HD, NQ), f32),
            jax.ShapeDtypeStruct((1, NQ), f32),
            slots,
            slots,
        ),
        in_specs=[VMEM] * 6,
        out_specs=(VMEM,) * 4 + (ANY,) * 2,
        scratch_shapes=[
            pltpu.VMEM((NQ, HD), bf16),
            pltpu.VMEM((1, NQ), f32),
            pltpu.VMEM((1, NQ), f32),
            pltpu.VMEM((HD, NQ), f32),
            pltpu.VMEM((HD, NQ), f32),
            *sems(110),
            pltpu.SemaphoreType.DMA((2,)),
        ],
        compiler_params=params(1),
    )(*arrays)


def mlp_kernel(*refs):
    attn_low, w_out, x, gain, gate_w, up_w, og, og_hbm, w_down_hbm = refs[:9]
    resid, grad_resid, gain_terms, up_terms, down_terms, gate_sum, down_sum = refs[9:16]
    pa, pb, wd, og_all, act_all, grad_hidden, hidden, ggp, gup, bk, dn, bk_core, dn_core, bk_sent, bk_in = refs[16:31]
    nb, rn, gate_terms, gate_in, send_sems, recv_sems, local_sems = refs[31:]
    me = here()
    z, y, c = me["z"], me["y"], me["c"]
    partner, other = at(me, c=1), at(me, n=1)
    ys = {d: at(me, y=d) for d in (1, 2, 3)}
    zs = {d: at(me, z=d) for d in (1, 2, 3)}
    greet([partner, other, *ys.values(), *zs.values()])
    copies = Copies(send_sems, recv_sems)
    units = pl.ds(pl.multiple_of((y * 2 + c) * UNITS, 16), UNITS)
    load_down = pltpu.make_async_copy(w_down_hbm.at[units], wd, local_sems.at[0])
    load_down.start()
    load_og = pltpu.make_async_copy(og_hbm, og_all, local_sems.at[1])
    load_og.start()
    pa[...] = nn(attn_low[...], w_out[...]).astype(bf16)
    swap = copies.send(pa, pb, other)
    load_down.wait()
    load_og.wait()
    pair = (2 * TOK, D)
    for yi in range(4):
        grad_hidden[yi] = nt(og_all[yi].reshape(pair), wd[...])
    swap.wait_recv()
    total = x[...].astype(f32) + (pa[...].astype(f32) + pb[...].astype(f32))
    resid[...] = total
    inverse = lax.rsqrt(jnp.mean(total * total, axis=-1, keepdims=True) + rms_eps)
    act_all[y, c] = (total * inverse * gain[...]).astype(bf16)

    own = act_all.at[y, c]
    far = {d: copies.send(own, own, ys[d]) for d in (1, 3)}
    to_core = {0: [copies.send(own, own, partner)]}
    bk_cores, dn_cores, bk_moves = {}, {}, {}

    def block(d):
        yi = step(me, "y", d)
        rows = act_all[yi].reshape(pair)
        gate = nn(rows, gate_w[...])
        up = nn(rows, up_w[...])
        sigmoid = 1.0 / (1.0 + jnp.exp(-gate))
        silu = gate * sigmoid
        grads = grad_hidden[yi]
        hidden[yi] = (silu * up).astype(bf16)
        ggp[yi] = (grads * up * (sigmoid * (1.0 + gate * (1.0 - sigmoid)))).astype(bf16)
        gup[yi] = (grads * silu).astype(bf16)
        both = nt(ggp[yi], gate_w[...]) + nt(gup[yi], up_w[...])
        bk[yi] = both.astype(bf16).reshape(2, TOK, D)
        bk_cores[d] = copies.send(bk.at[yi, 1 - c], bk_core.at[yi], partner)
        dn[yi] = nn(hidden[yi], wd[...]).astype(bf16).reshape(2, TOK, D)
        dn_cores[d] = copies.send(dn.at[yi, 1 - c], dn_core.at[yi], partner)

    def pass_block(d):
        yi = step(me, "y", d)
        bk_cores[d].wait_recv()
        bk_sent[yi] = (bk[yi, c].astype(f32) + bk_core[yi].astype(f32)).astype(bf16)
        if d:
            bk_moves[d] = copies.send(bk_sent.at[yi], bk_in.at[d - 1], ys[d])

    def sum_down(d):
        yi = step(me, "y", d)
        dn_cores[d].wait_recv()
        down_sum[yi] = (dn[yi, c].astype(f32) + dn_core[yi].astype(f32)).astype(bf16)

    half = TOK // 2
    low, high = pl.ds(0, half), pl.ds(half, half)
    to_core[0][0].wait_recv()
    block(0)
    relay = {}
    for d, rows in ((1, low), (3, high)):
        far[d].wait_recv()
        yi = lax.rem(y + (4 - d), 4)
        got = act_all.at[yi, c]
        relay[d] = copies.send(got.at[rows], got.at[rows], ys[d])
        to_core[4 - d] = [copies.send(got, got, partner)]
    to_core[3][0].wait_recv()
    block(3)
    pass_block(0)
    to_core[2] = []
    for d, rows in ((1, low), (3, high)):
        relay[d].wait_recv()
        got = act_all.at[step(me, "y", 2), c, rows]
        to_core[2].append(copies.send(got, got, partner))
    to_core[1][0].wait_recv()
    block(1)
    pass_block(3)
    for copy in to_core[2]:
        copy.wait_recv()
    block(2)
    pass_block(1)
    pass_block(2)

    everything = (GROUP * TOK, D)
    all_units = (GROUP * TOK, UNITS)
    gate_terms[...] = tn(ggp[...].reshape(all_units), act_all[...].reshape(everything)).astype(bf16)

    def z_cols(d):
        return pl.ds(pl.multiple_of(step(me, "z", d) * 384, 384), 384)

    gate_moves = {
        d: copies.send(gate_terms.at[:, z_cols(d)], gate_in.at[d - 1], zs[d]) for d in (1, 3, 2)
    }
    up_terms[...] = tn(gup[...].reshape(all_units), act_all[...].reshape(everything)).astype(bf16)
    back = bk_sent[y].astype(f32)
    for d in (1, 3, 2):
        bk_moves[d].wait_recv()
        back = back + bk_in[d - 1].astype(f32)
    nb[...] = back.astype(bf16)
    swap_back = copies.send(nb, rn, other)
    down_terms[...] = tn(hidden[...].reshape(all_units), og_all[...].reshape(everything)).astype(bf16)
    for d in range(4):
        sum_down(d)
    swap_back.wait_recv()
    grad_act = nb[...].astype(f32) + rn[...].astype(f32)
    normed = resid[...] * inverse
    gain_terms[...] = jnp.sum(grad_act * normed, axis=0, keepdims=True)
    grad_normed = grad_act * gain[...]
    inner = jnp.mean(grad_normed * normed, axis=-1, keepdims=True)
    grad_resid[...] = og[...].astype(f32) + inverse * (grad_normed - normed * inner)
    for d in (1, 3, 2):
        gate_moves[d].wait_recv()
    gate_sum[...] = (gate_terms[:, z_cols(0)].astype(f32) + three(gate_in)).T.astype(bf16)
    copies.finish()


def feed_forward(*arrays):
    rows = pltpu.VMEM((TOK, D), bf16)
    return pl.pallas_call(
        mlp_kernel,
        out_shape=[
            jax.ShapeDtypeStruct((TOK, D), f32),
            jax.ShapeDtypeStruct((TOK, D), f32),
            jax.ShapeDtypeStruct((1, D), f32),
            jax.ShapeDtypeStruct((UNITS, D), bf16),
            jax.ShapeDtypeStruct((UNITS, D), bf16),
            jax.ShapeDtypeStruct((D // 4, UNITS), bf16),
            jax.ShapeDtypeStruct((4, TOK, D), bf16),
        ],
        in_specs=[VMEM] * 7 + [ANY] * 2,
        out_specs=[VMEM] * 7,
        scratch_shapes=[
            rows,
            rows,
            pltpu.VMEM((UNITS, D), bf16),
            pltpu.VMEM((4, 2, TOK, D), bf16),
            pltpu.VMEM((4, 2, TOK, D), bf16),
            pltpu.VMEM((4, 2 * TOK, UNITS), f32),
            *[pltpu.VMEM((4, 2 * TOK, UNITS), bf16)] * 3,
            *[pltpu.VMEM((4, 2, TOK, D), bf16)] * 2,
            *[pltpu.VMEM((4, TOK, D), bf16)] * 3,
            pltpu.VMEM((3, TOK, D), bf16),
            rows,
            rows,
            pltpu.VMEM((UNITS, D), bf16),
            pltpu.VMEM((3, UNITS, D // 4), bf16),
            *sems(40),
            pltpu.SemaphoreType.DMA((2,)),
        ],
        compiler_params=params(2),
    )(*arrays)


def back_kernel(*refs):
    (q_in, kv, exact, start, ids, lse, grad_resid, w_out, attn_low, cosine, sine, normed, inverse) = refs[:13]
    gain, resid, mlp_gain_terms, gate_sum, w_qkv_hbm, act_hbm, *terms, down_terms = refs[13:22]
    in_grad, layer_out, sum_gate, sum_up, sum_down, sum_qkv, sum_out, small_out = refs[22:30]
    (q, g, acc, dkv, cb, s, r1a, r1b, ta, tb, r2a, r2b, u, r3, w_qkv, act_all, gb_all, al_heads, al_all) = refs[30:49]
    gp, gp_flat, gp_all, part, part_other, small, e1, e2, e3, f1, f2 = refs[49:60]
    own, first_in, mid = refs[60:62], refs[62:64], refs[64:66]
    second_in, summed, third_in = (refs[66 + 3 * k : 69 + 3 * k] for k in range(3))
    q_terms, q_first, q_mid, q_second, q_summed, q_third = refs[75:81]
    down_own, down_in, down_part, down_other, send_sems, recv_sems, local_sems = refs[81:]

    me = here()
    z, y, xh, c, n = (me[a] for a in AXES)
    partner, across, other = at(me, c=1), at(me, xh=1), at(me, n=1)
    ys = {d: at(me, y=d) for d in (1, 2, 3)}
    zs = {d: at(me, z=d) for d in (1, 2, 3)}
    near_moves = [(d, e) for d in (1, 3, 2, 0) for e in (0, 1) if d or e]
    near = {m: at(me, y=m[0], xh=m[1]) for m in near_moves}
    group = {m: at(me, y=m[0], c=m[1]) for m in near_moves}
    greet([other, *zs.values(), *near.values(), *(group[m] for m in near_moves if m[1])])
    copies = Copies(send_sems, recv_sems)
    half = TOK // 2
    low, high = pl.ds(0, half), pl.ds(half, half)

    local = []

    def load(src, dst):
        copy = pltpu.make_async_copy(src, dst, local_sems.at[len(local)])
        copy.start()
        local.append(copy)
        return copy

    def z_cols(d):
        return pl.ds(pl.multiple_of(step(me, "z", d) * 384, 384), 384)

    second = {}

    def send_second(i, source, in_ref):
        for m in near_moves:
            second[i, m] = copies.send(
                source(step(me, "y", m[0]), step(me, "xh", m[1])), in_ref.at[y, xh], near[m]
            )

    def strip(yi, xi):
        return pl.ds(pl.multiple_of(96 * yi + 48 * xi, 48), 48)

    send_second(0, lambda yi, xi: gate_sum.at[strip(yi, xi)], second_in[0])
    second_in[0][y, xh] = gate_sum[strip(y, xh), :]
    first = {}

    def send_first(i, d):
        first[i, d] = copies.send(terms[i].at[:, z_cols(d)], first_in[i].at[d - 1], zs[d])

    for d in (1, 3, 2):
        send_first(0, d)
    for d in (1, 3):
        send_first(1, d)

    gb_all[y, c] = grad_resid[...].astype(bf16)
    branch = gb_all[y, c]
    branches = Rows(me, copies, gb_all.at[y, c], gb_all)
    down_moves = {
        d: copies.send(down_terms.at[step(me, "y", d)], down_in.at[d - 1], ys[d]) for d in (1, 3, 2)
    }
    load_down = load(down_terms.at[y], down_own)
    for h in range(HEADS):
        al_heads[h] = attn_low[:, pl.ds(h * HD, HD)]

    def head_of(d, e):
        taker = step(me, "y", d) * 2 + step(me, "c", e)
        return jnp.where(taker < HEADS, taker, 0)

    al_moves = [
        copies.send(al_heads.at[head_of(*m)], al_all.at[y, c], group[m]) for m in near_moves
    ]
    al_all[y, c] = al_heads[head_of(0, 0)]
    load_w = load(w_qkv_hbm, w_qkv)
    load_act = load(act_hbm, act_all)
    load_own = [load(terms[i].at[:, z_cols(0)], own[i]) for i in range(2)]

    heads_in(q_in, q)
    grads_in = nt(branch, w_out[...]).astype(bf16)
    for h in range(HEADS):
        g[pl.ds(h * TOK, TOK), :] = grads_in[:, h * HD : (h + 1) * HD]
    balance = jnp.sum(g[...].astype(f32).T * exact[...], axis=0, keepdims=True)
    acc[...] = jnp.zeros_like(acc)
    last = shard_of(me) // BLOCK_SHARDS
    log_total = lse[...]
    earlier = jnp.where(start[...] < last * KEY_BLOCK, log_total, -big_negative)

    def block(index, masked, shift):
        zi, yi = index // 4, lax.rem(index, 4)
        shape = (2, 2, TOK, HD)
        keys = kv[zi, yi, :, :, :, pl.ds(0, HD)].reshape(KEY_BLOCK, HD)
        values = kv[zi, yi, :, :, :, pl.ds(HD, HD)].reshape(KEY_BLOCK, HD)
        keys_t = keys.T
        dk = jnp.zeros((KEY_BLOCK, HD), f32)
        dv = jnp.zeros((KEY_BLOCK, HD), f32)
        for chunk in range(NQ // Q_CHUNK):
            cs = pl.ds(chunk * Q_CHUNK, Q_CHUNK)
            piece = slice(chunk * Q_CHUNK, (chunk + 1) * Q_CHUNK)
            qc, gc = q[cs, :], g[cs, :]
            probs = jnp.exp2(nt(keys, qc) * SCALE_LOG2 - shift[:, piece])
            if masked:
                key_ids = index * KEY_BLOCK + lax.broadcasted_iota(jnp.int32, (KEY_BLOCK, Q_CHUNK), 0)
                allowed = (key_ids >= start[:, cs]) & (key_ids <= ids[:, cs])
                probs = jnp.where(allowed, probs, 0.0)
            grads = (probs * (nt(values, gc) - balance[:, piece])).astype(bf16)
            dv = dv + nn(probs.astype(bf16), gc)
            dk = dk + nn(grads, qc)
            acc[:, cs] = acc[:, cs] + nn(keys_t, grads)
        dkv[zi, yi, :, :, :, pl.ds(0, HD)] = (dk * SCALE).astype(bf16).reshape(shape)
        dkv[zi, yi, :, :, :, pl.ds(HD, HD)] = dv.astype(bf16).reshape(shape)

    middle = (last + 1) // 2

    @pl.when(last > 0)
    def _():
        block(0, True, earlier)

    @pl.loop(1, middle)
    def _(index):
        block(index, False, earlier)

    branches.pass_on()

    @pl.loop(jnp.maximum(middle, 1), last)
    def _(index):
        block(index, False, earlier)

    block(last, True, log_total)

    @pl.loop(last + 1, TOKENS // KEY_BLOCK)
    def _(index):
        dkv[index // 4, lax.rem(index, 4)] = jnp.zeros((2, 2, TOK, 2 * HD), bf16)

    kv_cores = [
        copies.send(dkv.at[:, :, :, 1 - c, rows], cb.at[:, :, :, rows], partner)
        for rows in (low, high)
    ]
    first_a, first_b, second_a, second_b = {}, {}, {}, {}
    for rows, core in ((low, kv_cores[0]), (high, kv_cores[1])):
        core.wait_recv()
        for zi in range(4):
            s[zi, :, :, rows] = (dkv[zi, :, :, c, rows].astype(f32) + cb[zi, :, :, rows].astype(f32)).astype(bf16)
        for d in (1, 3, 2):
            if rows is low:
                first_a[d] = copies.send(s.at[step(me, "z", d), :, :, low], r1a.at[d - 1], zs[d])
            else:
                first_b[d] = copies.send(s.at[:, step(me, "y", d), :, high], r1b.at[d - 1], ys[d])

    send_first(1, 2)
    load_down.wait()
    mlp_out = down_own[...].astype(f32)
    for d in (1, 3, 2):
        down_moves[d].wait_recv()
        mlp_out = mlp_out + down_in[d - 1].astype(f32)
    down_part[...] = mlp_out.astype(bf16)
    down_swap = copies.send(down_part, down_other, other)
    turned_back = (acc[...] * SCALE).T

    def revert(rows):
        return rows * cosine[...] - pltpu.roll(rows, HD // 2, 1) * sine[...]

    def keep_head(h, rows):
        low_rows = rows.astype(bf16)
        gp[h] = low_rows
        gp_flat[:, pl.ds(h * HD, HD)] = low_rows
        small[pl.ds(2, 1), pl.ds(h * HD, HD)] = jnp.sum(low_rows.astype(f32), axis=0, keepdims=True)

    small[...] = jnp.zeros_like(small)
    small[pl.ds(1, 1), :] = mlp_gain_terms[...]
    for h in range(HEADS):
        keep_head(h, revert(turned_back[h * TOK : (h + 1) * TOK]))
    load_w.wait()
    front = HEADS * HD
    partial = nt(gp_flat[:, pl.ds(0, front)], w_qkv[:, pl.ds(0, front)])

    for d in (1, 3, 2):
        first_a[d].wait_recv()
    ta[...] = (s[z, :, :, low].astype(f32) + three(r1a)).astype(bf16)
    for d in (1, 3, 2):
        second_a[d] = copies.send(ta.at[step(me, "y", d)], r2a.at[d - 1], ys[d])
    for d in (1, 3, 2):
        first_b[d].wait_recv()
    tb[...] = (s[:, y, :, high].astype(f32) + three(r1b)).astype(bf16)
    for d in (1, 3, 2):
        second_b[d] = copies.send(tb.at[step(me, "z", d)], r2b.at[d - 1], zs[d])
    for d in (1, 3, 2):
        second_a[d].wait_recv()
        second_b[d].wait_recv()
    ua = ta[y].astype(f32) + three(r2a)
    ub = tb[z].astype(f32) + three(r2b)
    u[:, low] = ua.astype(bf16)
    u[:, high] = ub.astype(bf16)
    kv_last = copies.send(u.at[1 - xh], r3, across)

    branches.complete()
    kv_last.wait_recv()
    grad_kv = u[xh].astype(f32) + r3[...].astype(f32)
    keep_head(HEADS, revert(grad_kv[:, :HD]))
    keep_head(HEADS + 1, grad_kv[:, HD:])
    gp_moves = [
        copies.send(gp.at[step(me, "y", m[0]) * 2 + step(me, "c", m[1])], gp_all.at[y, c], group[m])
        for m in near_moves
    ]
    gp_all[y, c] = gp[y * 2 + c]
    back = pl.ds(front, 2 * HD)
    part[...] = (partial + nt(gp_flat[:, back], w_qkv[:, back])).astype(bf16)
    swap = copies.send(part, part_other, other)
    load_act.wait()
    for copy in gp_moves:
        copy.wait_recv()
    q_terms[pl.ds(0, HD), :] = tn(
        gp_all[...].reshape(GROUP * TOK, HD), act_all[...].reshape(GROUP * TOK, D)
    ).astype(bf16)

    q_one = {d: copies.send(q_terms.at[pl.ds(0, HD), z_cols(d)], q_first.at[d - 1, pl.ds(0, HD)], zs[d]) for d in (1, 3, 2)}
    branches.wait()
    for copy in al_moves:
        copy.wait_recv()
    q_terms[pl.ds(HD, HD), :] = tn(
        al_all[...].reshape(GROUP * TOK, HD), gb_all[...].reshape(GROUP * TOK, D)
    ).astype(bf16)
    q_two = {d: copies.send(q_terms.at[pl.ds(HD, HD), z_cols(d)], q_first.at[d - 1, pl.ds(HD, HD)], zs[d]) for d in (1, 3, 2)}

    swap.wait_recv()
    grad_act = part[...].astype(f32) + part_other[...].astype(f32)
    small[pl.ds(0, 1), :] = jnp.sum(grad_act * normed[...], axis=0, keepdims=True)
    small_one = {d: copies.send(small, e1.at[d - 1], zs[d]) for d in (1, 3, 2)}
    grad_normed = grad_act * gain[...]
    inner = jnp.mean(grad_normed * normed[...], axis=-1, keepdims=True)
    in_grad[...] = (grad_resid[...] + inverse[...] * (grad_normed - normed[...] * inner)).astype(bf16)

    for d in (1, 3, 2):
        small_one[d].wait_recv()
    f1[...] = small[...] + three(e1)
    small_two = {m: copies.send(f1, e2.at[k], near[m]) for k, m in enumerate(near_moves)}
    def send_mid(i, total, mid_ref, in_ref):
        turned = total.T.astype(bf16)
        for yi in range(4):
            for xi in range(2):
                rows = 96 * yi + 48 * xi
                mid_ref[yi, xi] = turned[rows : rows + 48]
        send_second(i, lambda yi, xi: mid_ref.at[yi, xi], in_ref)
        in_ref[y, xh] = mid_ref[y, xh]

    for i in range(2):
        load_own[i].wait()
        for d in (1, 3, 2):
            first[i, d].wait_recv()
        send_mid(i + 1, own[i][...].astype(f32) + three(first_in[i]), mid[i], second_in[i + 1])
    for d in (1, 3, 2):
        q_one[d].wait_recv()
        q_two[d].wait_recv()
    send_mid(3, q_terms[:, z_cols(0)].astype(f32) + three(q_first), q_mid, q_second)

    for m in near_moves:
        small_two[m].wait_recv()
    f2[...] = f1[...]
    for k in range(len(near_moves)):
        f2[...] = f2[...] + e2[k]
    small_three = copies.send(f2, e3, partner)
    keep, give = pl.ds(pl.multiple_of(24 * c, 8), 24), pl.ds(pl.multiple_of(24 * (1 - c), 8), 24)
    third = []
    all_summed = [*summed, q_summed]
    all_second = [*second_in, q_second]
    all_third = [*third_in, q_third]
    for i in range(4):
        for m in near_moves:
            second[i, m].wait_recv()
        all_summed[i][...] = all_second[i][:, 0].astype(f32) + all_second[i][:, 1].astype(f32)
        third.append(copies.send(all_summed[i].at[:, give], all_third[i], partner))
    for i, outs in enumerate(((sum_gate,), (sum_up,), (sum_down,), (sum_qkv, sum_out))):
        third[i].wait_recv()
        for yi in range(4):
            mine_sum, their_sum = all_summed[i][yi, keep], all_third[i][yi]
            pair = (jnp.where(c == 0, mine_sum, their_sum), jnp.where(c == 0, their_sum, mine_sum))
            for e in range(2):
                k = 2 * yi + e
                if i < 3:
                    outs[0][:, pl.ds(k * UNITS, UNITS)] = pair[e]
                else:
                    outs[0][:, pl.ds(k * HD, HD)] = pair[e][:, :HD]
                    if k < HEADS:
                        outs[1][:, pl.ds(k * HD, HD)] = pair[e][:, HD:]
    small_three.wait_recv()
    small_out[...] = f2[...] + e3[...]
    down_swap.wait_recv()
    layer_out[...] = (
        resid[...] + (down_part[...].astype(f32) + down_other[...].astype(f32))
    ).astype(bf16)
    copies.finish()


def back(*arrays):
    half = TOK // 2
    wide = 2 * HD
    return pl.pallas_call(
        back_kernel,
        out_shape=[
            jax.ShapeDtypeStruct((TOK, D), bf16),
            jax.ShapeDtypeStruct((TOK, D), bf16),
            *[jax.ShapeDtypeStruct((24, FF // 2), f32)] * 3,
            jax.ShapeDtypeStruct((24, (HEADS + 2) * HD), f32),
            jax.ShapeDtypeStruct((24, HEADS * HD), f32),
            jax.ShapeDtypeStruct((8, D), f32),
        ],
        in_specs=[VMEM] * 17 + [ANY] * 5,
        out_specs=[VMEM] * 8,
        scratch_shapes=[
            pltpu.VMEM((NQ, HD), bf16),
            pltpu.VMEM((NQ, HD), bf16),
            pltpu.VMEM((HD, NQ), f32),
            pltpu.VMEM((4, 4, 2, 2, TOK, wide), bf16),
            pltpu.VMEM((4, 4, 2, TOK, wide), bf16),
            pltpu.VMEM((4, 4, 2, TOK, wide), bf16),
            pltpu.VMEM((3, 4, 2, half, wide), bf16),
            pltpu.VMEM((3, 4, 2, half, wide), bf16),
            pltpu.VMEM((4, 2, half, wide), bf16),
            pltpu.VMEM((4, 2, half, wide), bf16),
            pltpu.VMEM((3, 2, half, wide), bf16),
            pltpu.VMEM((3, 2, half, wide), bf16),
            pltpu.VMEM((2, TOK, wide), bf16),
            pltpu.VMEM((TOK, wide), bf16),
            pltpu.VMEM((D, (HEADS + 2) * HD), bf16),
            pltpu.VMEM((4, 2, TOK, D), bf16),
            pltpu.VMEM((4, 2, TOK, D), bf16),
            pltpu.VMEM((HEADS, TOK, HD), bf16),
            pltpu.VMEM((4, 2, TOK, HD), bf16),
            pltpu.VMEM((HEADS + 2, TOK, HD), bf16),
            pltpu.VMEM((TOK, (HEADS + 2) * HD), bf16),
            pltpu.VMEM((4, 2, TOK, HD), bf16),
            pltpu.VMEM((TOK, D), bf16),
            pltpu.VMEM((TOK, D), bf16),
            pltpu.VMEM((8, D), f32),
            pltpu.VMEM((3, 8, D), f32),
            pltpu.VMEM((7, 8, D), f32),
            pltpu.VMEM((8, D), f32),
            pltpu.VMEM((8, D), f32),
            pltpu.VMEM((8, D), f32),
            *[pltpu.VMEM((UNITS, 384), bf16)] * 2,
            *[pltpu.VMEM((3, UNITS, 384), bf16)] * 2,
            *[pltpu.VMEM((4, 2, 48, UNITS), bf16)] * 2,
            *[pltpu.VMEM((4, 2, 48, UNITS), bf16)] * 3,
            *[pltpu.VMEM((4, 48, UNITS), f32)] * 3,
            *[pltpu.VMEM((4, 24, UNITS), f32)] * 3,
            pltpu.VMEM((wide, D), bf16),
            pltpu.VMEM((3, wide, 384), bf16),
            pltpu.VMEM((4, 2, 48, wide), bf16),
            pltpu.VMEM((4, 2, 48, wide), bf16),
            pltpu.VMEM((4, 48, wide), f32),
            pltpu.VMEM((4, 24, wide), f32),
            pltpu.VMEM((TOK, D), bf16),
            pltpu.VMEM((3, TOK, D), bf16),
            pltpu.VMEM((TOK, D), bf16),
            pltpu.VMEM((TOK, D), bf16),
            *sems(140),
            pltpu.SemaphoreType.DMA((9,)),
        ],
        compiler_params=params(9, 62),
    )(*arrays)


def row_starts(lengths, token_ids):
    ends = jnp.cumsum(lengths)
    before = ends[None, :] <= token_ids[:, None]
    return jnp.sum(jnp.where(before, lengths[None, :], 0), axis=1)


def rope_tables(positions):
    half = HD // 2
    freqs = rope_base ** (-2.0 * jnp.arange(half, dtype=f32) / HD)
    angles = positions.astype(f32)[:, None] * freqs[None, :]
    cosine, sine = jnp.cos(angles), jnp.sin(angles)
    return jnp.concatenate([cosine, cosine], 1), jnp.concatenate([-sine, sine], 1)


def rotate(values, cosine, sine):
    heads = []
    for h in range(values.shape[1] // HD):
        one = values[:, h * HD : (h + 1) * HD]
        swapped = jnp.concatenate([one[:, HD // 2 :], one[:, : HD // 2]], axis=1)
        heads.append(one * cosine + swapped * sine)
    return jnp.concatenate(heads, axis=1)


def normalize(values):
    inverse = lax.rsqrt(jnp.mean(values * values, axis=-1) + rms_eps)
    return (values * inverse[:, None], inverse)


def shards(
    layer_in, lengths, norm_attn, w_qkv, qkv_bias, w_out, norm_mlp, w_gate, w_up, w_down, out_grad
):
    shard = lax.axis_index(WIDE)
    member = lax.axis_index(("y", "c"))
    own_ids = shard * TOK + jnp.arange(TOK, dtype=jnp.int32)
    seq_starts = row_starts(lengths, own_ids)
    cosine, sine = rope_tables(own_ids - seq_starts)
    start = jnp.tile(seq_starts, HEADS)[None]
    ids = jnp.tile(own_ids, HEADS)[None]
    gate_w = lax.dynamic_slice(w_gate, (0, member * UNITS), (D, UNITS))
    up_w = lax.dynamic_slice(w_up, (0, member * UNITS), (D, UNITS))

    input_f32 = layer_in.astype(f32)
    normed_attn, inverse_attn = normalize(input_f32)
    act_attn = (normed_attn * norm_attn).astype(bf16)
    projected = nn(act_attn, w_qkv) + qkv_bias[0]
    turned = rotate(projected[:, : (HEADS + 1) * HD], cosine, sine).astype(bf16)
    queries = turned[:, : HEADS * HD]
    kv_own = jnp.concatenate(
        [turned[:, HEADS * HD :], projected[:, (HEADS + 1) * HD :].astype(bf16)], axis=1
    )
    kv, attn_low, exact, lse, out_grad_all, act_attn_all = attend(
        kv_own, queries, start, ids, out_grad, act_attn
    )
    resid, grad_resid, gain_terms, up_terms, down_terms, gate_sum, down_sum = feed_forward(
        attn_low, w_out, layer_in, norm_mlp[None], gate_w, up_w, out_grad, out_grad_all, w_down
    )
    in_grad, layer_out, sum_gate, sum_up, sum_down, sum_qkv, sum_out, small = back(
        queries, kv, exact, start, ids, lse, grad_resid, w_out, attn_low, cosine, sine, normed_attn,
        inverse_attn[:, None], norm_attn[None], resid, gain_terms, gate_sum,
        w_qkv, act_attn_all, up_terms, down_terms, down_sum,
    )
    norms = lax.dynamic_slice(small, (0, shard * 24), (2, 24))
    bias = lax.dynamic_slice(
        small[2, : (HEADS + 2) * HD].reshape(HEADS + 2, HD), (0, shard * 2), (HEADS + 2, 2)
    )
    return (
        layer_out,
        in_grad,
        norms[0],
        sum_qkv,
        bias[None, : HEADS + 1],
        bias[HEADS + 1 :],
        sum_out.T,
        norms[1],
        sum_gate,
        sum_up,
        sum_down.T,
    )


def solution(mesh):
    torus = Mesh(mesh.devices.reshape(4, 4, 2, 2, 2), AXES)
    in_specs = (
        P(WIDE, None),
        P(),
        P(),
        P(None, "n"),
        P("n", None),
        P("n", None),
        P(),
        P(None, "n"),
        P(None, "n"),
        P("n", None),
        P(WIDE, None),
    )
    out_specs = (
        P(WIDE, None),
        P(WIDE, None),
        P(WIDE),
        P(WIDE, "n"),
        P("n", None, WIDE),
        P("n", WIDE),
        P("n", WIDE),
        P(WIDE),
        P(WIDE, "n"),
        P(WIDE, "n"),
        P("n", WIDE),
    )
    return jax.shard_map(
        shards, mesh=torus, in_specs=in_specs, out_specs=out_specs, check_vma=False
    )
```

time: 400 us -> 291 us (0.73)
  Pallas kernels: 307 us -> 252 us
  matrix products: 48.3 us -> 2.61 us
  other arithmetic: 13.5 us -> 7.33 us
    pallas_call x1, Pallas kernels: 161 us -> 112 us  [back(): pl.pallas_call(back_kernel, out_shape=[jax.ShapeDtypeStruct((TOK, D), bf1...]
    dot_general x6 -> x0, matrix products: 26.9 us -> none  [the longest x3 16.6 us: nt(): lax.dot_general(a, b, (((1,), (1,)), ((), ())), preferred_element_type=f32)]
    dot_general x5 -> x1, matrix products: 21.4 us -> 2.61 us  [nn(): lax.dot_general(a, b, (((1,), (0,)), ((), ())), preferred_element_type=f32)]
    convert_element_type x3 -> x0, local copies, waits for them, and re-layouts: 7.08 us -> none  [shards(): t.astype(bf16)]
    dynamic_slice x0 -> x1, local copies, waits for them, and re-layouts: none -> 6.6 us  [shards(): up_w = lax.dynamic_slice(w_up, (0, member * UNITS), (D, UNITS))]
    pallas_call x5 -> x2, Pallas kernels: 146 us -> 141 us  [the longest x1 72.3 us: feed_forward(): pl.pallas_call(mlp_kernel, out_shape=[jax.ShapeDtypeStruct((TOK, D), f32)...]
    unnamed x41 -> x23, local copies, waits for them, and re-layouts: 11 us -> 9.94 us
where the time goes in v3:
time: 291 us; the launch traced here: 286 us
  Pallas kernels  252 us (87%)
  local copies, waits for them, and re-layouts  22.4 us (8%)
  other arithmetic  7.33 us (3%)
    pallas_call x1, Pallas kernels, back(): pl.pallas_call(back_kernel, out_shape=[jax.ShapeDtypeStruct((TOK, D), bf1...  112 us
    pallas_call x1, Pallas kernels, feed_forward(): pl.pallas_call(mlp_kernel, out_shape=[jax.ShapeDtypeStruct((TOK, D), f32)...  72.3 us
    pallas_call x1, Pallas kernels, attend(): pl.pallas_call(attend_kernel, out_shape=(jax.ShapeDtypeStruct((4, 4, 2, 2...  68.3 us
    unnamed x23, local copies, waits for them, and re-layouts  9.94 us
    dynamic_slice x1, local copies, waits for them, and re-layouts, shards(): up_w = lax.dynamic_slice(w_up, (0, member * UNITS), (D, UNITS))  6.6 us

profile of v3, /device:TPU:1, one launch (start us, length us, event | category | flops | bytes accessed | tf_op | source)
XLA Modules:
  0.0 286.0 jit_solution(5093377950775607680)
XLA Ops:
  0.7 0.8 reduce-window.8
  1.5 0.7 select_reduce_fusion
  2.2 1.2 fusion
  3.4 2.1 convert_multiply_fusion
  5.5 2.6 convolution_add_fusion
  8.5 0.8 fusion.2
  10.0 0.7 pad_maximum_fusion.2.x
  11.3 68.3 %shard_map.194 = (bf16[4,4,2,2,128,256]{5,4,3,2,1,0:T(8,128)(2,1)}, bf16[128,768]{1,0:T(8,128)(2,1)}, f32[128,768]{1,0:T(8,128)}, f32[1,768]{1,0:T(1,128)}, bf16...) custom-call(bf16[128,256]{1,0:T(8,128)(2,1)} %pad_maximum_fusion.2.x, bf16[128,768]{1,0:T(8,128)(2,1)} %copy-done.2, ...), custom_call_target="tpu_custom_call" | custom-call | tf_op jit(solution)/shard_map/pallas_call | solution.py:291
  79.6 6.6 %constant_dynamic-slice_fusion.1 = (bf16[1536,560]{1,0:T(8,128)(2,1)}, bf16[1536,560]{1,0:T(8,128)(2,1)}) fusion(bf16[1536,4480]{1,0:T(8,128)(2,1)} %param.19, s32[]{:T(128)S(6)} %select_n.15, bf16[1536,4480]{1,0:T(8,128)(2,1)} %param.18), kind=kLoop, calls=%fused_computation.52 | loop fusion | bytes 6881284 | tf_op jit(solution)/shard_map/dynamic_slice | solution.py:881
  86.2 0.6 broadcast_in_dim.31.refs_3_
  86.8 72.3 %shard_map.195 = (f32[128,1536]{1,0:T(8,128)}, f32[128,1536]{1,0:T(8,128)}, f32[1,1536]{1,0:T(1,128)}, bf16[560,1536]{1,0:T(8,128)(2,1)}, bf16[560,1536]{1,0:T(8...) custom-call(bf16[128,768]{1,0:T(8,128)(2,1)} %get-tuple-element.35.refs_0_.refs_8_, ...), custom_call_target="tpu_custom_call" | custom-call | tf_op jit(solution)/shard_map/pallas_call | solution.py:443
  159.1 0.7 copy.24.refs_12_
  159.9 0.6 broadcast_in_dim.32.refs_13_
  160.5 111.8 %shard_map.196 = (bf16[128,1536]{1,0:T(8,128)(2,1)}, bf16[128,1536]{1,0:T(8,128)(2,1)}, f32[24,4480]{1,0:T(8,128)}, f32[24,4480]{1,0:T(8,128)}, f32[24,4480]{1,0...) custom-call(bf16[128,768]{1,0:T(8,128)(2,1)} %copy-done.2, ...), custom_call_target="tpu_custom_call" | custom-call | tf_op jit(solution)/shard_map/pallas_call | solution.py:776
  272.3 0.8 slice.133
  273.2 0.7 copy.25
  274.4 0.8 constant_dynamic-slice_fusion
  275.7 1.8 copy.42
  277.5 1.8 copy.43
  279.2 1.5 copy.44
  280.8 1.5 copy.45
  282.3 1.8 copy.46
  284.1 0.8 copy.47
  284.8 0.8 copy.48
  (31 shorter events, 2.8 us)
Async XLA Ops:
  5.5 3.7 %copy-start.1 = (bf16[128,1536]{1,0:T(8,128)(2,1)}, bf16[128,1536]{1,0:T(8,128)(2,1)S(1)}, u32[]{:S(2)}) copy-start(bf16[128,1536]{1,0:T(8,128)(2,1)S(1)} %get-tuple-element.72.aa) | copy-start | bytes 1179652
  9.2 77.0 %copy-start = (f32[128,128]{1,0:T(8,128)}, f32[128,128]{1,0:T(8,128)S(1)}, u32[]{:S(2)}) copy-start(f32[128,128]{1,0:T(8,128)S(1)} %get-tuple-element.54.refs_10_) | copy-start | bytes 196612
  10.0 1.3 copy-start.2
  79.6 6.6 %copy-start.6 = (f32[1536]{0:T(1024)S(1)}, f32[1536]{0:T(1024)}, u32[]{:S(2)}) copy-start(f32[1536]{0:T(1024)} %param.17) | copy-start | bytes 18436
  86.8 73.1 %copy-start.5 = (f32[1536]{0:T(1024)S(1)}, f32[1536]{0:T(1024)}, u32[]{:S(2)}) copy-start(f32[1536]{0:T(1024)} %param.13) | copy-start | bytes 18436
  272.3 11.8 %copy-start.4 = (f32[24,4480]{1,0:T(8,128)S(1)}, f32[24,4480]{1,0:T(8,128)}, u32[]{:S(2)}) copy-start(f32[24,4480]{1,0:T(8,128)} %get-tuple-element.119) | copy-start | bytes 1290244
  272.3 12.5 %copy-start.3 = (f32[24,4480]{1,0:T(8,128)S(1)}, f32[24,4480]{1,0:T(8,128)}, u32[]{:S(2)}) copy-start(f32[24,4480]{1,0:T(8,128)} %get-tuple-element.52) | copy-start | bytes 1290244
